TPU v7x, 256 devices: a whole 4x4x8 slice. The times are simulated.
256 devices in a mesh: dp: 8 (over x, core), seq: 32 (over z, y).
Axes of the slice: x: 4, y: 4, z: 8, core: 2. Of those that a mesh axis runs over, the one named last changes fastest.
Arguments:
- activations: bfloat16 [4, 16384, 6144], P(None, ('dp', 'seq')), may hold values from -16 to 16
- prev_basis: bfloat16 [4, 1536, 512], replicated, may hold values from -0.15625 to 0.15625
Outputs:
- new_basis: float32 [6144, 512], P('seq')
All inputs are finite; a program needn't handle non-finite values.
Results may differ from a plain program's by a relative error of at most 0.0085.
Values may be sent and summed in bfloat16 or wider, within the bound.
A program may use at most 128 MiB of HBM per device.

v0:
```python
import math

import jax
import jax.numpy as jnp
from jax import lax
from jax.sharding import PartitionSpec as P


def swapped(value, axis, bit):
    mask = 2**bit
    pairs = [(source, source ^ mask) for source in range(lax.axis_size(axis))]
    return lax.ppermute(value, axis, pairs)


def contract_rows(left_side, right_side):
    return lax.dot_general(
        left_side, right_side, (((0,), (0,)), ((), ())), preferred_element_type=jnp.float32
    )


def on_device(activations, prev_basis):
    blocks = prev_basis.shape[0]
    block_width = prev_basis.shape[1]
    basis_cols = prev_basis.shape[2]
    micro_count = activations.shape[0]
    seq_count = lax.axis_size("seq")
    groups = seq_count // blocks
    group_bits = groups.bit_length() - 1
    position = lax.axis_index("seq")
    member = position % groups
    token_total = micro_count * activations.shape[1] * lax.axis_size("dp") * seq_count
    block_basis = lax.dynamic_index_in_dim(prev_basis, position // groups, 0, keepdims=False)
    partial_sum = jnp.zeros((block_width, basis_cols), jnp.float32)
    for micro_idx in range(micro_count):
        token_rows = activations[micro_idx]
        per_group = token_rows.shape[0] // groups
        outgoing = token_rows.reshape(groups, per_group, blocks, block_width)
        outgoing = outgoing.transpose(2, 0, 1, 3).reshape(seq_count, per_group, block_width)
        arrived = lax.all_to_all(outgoing, "seq", split_axis=0, concat_axis=1, tiled=True).reshape(
            -1, block_width
        )
        projected = jnp.dot(arrived, block_basis, preferred_element_type=jnp.float32).astype(
            jnp.bfloat16
        )
        partial_sum = partial_sum + contract_rows(arrived, projected)
    partial_sum = lax.psum(partial_sum, "dp")
    for bit_pos in reversed(range(group_bits)):
        half_rows = partial_sum.shape[0] // 2
        upper_half = member // (1 << bit_pos) % 2
        kept_half = lax.dynamic_slice_in_dim(partial_sum, upper_half * half_rows, half_rows, 0)
        handed = lax.dynamic_slice_in_dim(partial_sum, (1 - upper_half) * half_rows, half_rows, 0)
        partial_sum = kept_half + swapped(handed, "seq", bit_pos)
    panel = partial_sum / token_total
    gram_small = jnp.dot(panel.T, panel, precision=lax.Precision.HIGHEST)
    for bit_pos in range(group_bits):
        gram_small = gram_small + swapped(gram_small, "seq", bit_pos)
    factor = jnp.linalg.cholesky(gram_small)
    solved = jax.scipy.linalg.solve_triangular(factor, panel.T, lower=True)
    return solved.T * math.sqrt(block_width)


def solution(mesh):
    in_specs = (P(None, ("dp", "seq"), None), P())
    out_specs = P("seq", None)
    return jax.shard_map(
        on_device, mesh=mesh, in_specs=in_specs, out_specs=out_specs, check_vma=False
    )
```

profile of v0, /device:TPU:6, one launch (start us, length us, event | category | flops | bytes accessed | tf_op | source)
XLA Modules:
  0.0 496.1 jit_solution(4497870032698211639)
XLA Ops:
  6.5 2.0 fusion.98
  8.6 1.5 reshape_squeeze.12
  10.1 2.2 copy.9
  12.2 11.5 %all-to-all-start = ((bf16[32,8,1536]{2,1,0:T(8,128)(2,1)}), bf16[32,8,1536]{2,1,0:T(8,128)(2,1)S(1)}, u32[]{:S(2)}, u32[]{:S(2)}) async-start(bf16[32,8,1536]{2,1,0:T(8,128)(2,1)} %bitcast.101), calls=%async_computation | async-start | bytes 1572864 | tf_op jit(solution)/shard_map/all_to_all | solution.py:39
  23.7 1.5 reshape_squeeze.13
  25.2 2.2 copy.10
  27.3 19.3 %all-to-all-done = bf16[32,8,1536]{2,1,0:T(8,128)(2,1)S(1)} async-done(((bf16[32,8,1536]{2,1,0:T(8,128)(2,1)}), bf16[32,8,1536]{2,1,0:T(8,128)(2,1)S(1)}, u32[]{:S(2)}, u32[]{:S(2)}) %all-to-all-start) | async-done | bytes 786464 | tf_op jit(solution)/shard_map/all_to_all | solution.py:39
  46.6 5.1 %all-to-all-start.1 = ((bf16[32,8,1536]{2,1,0:T(8,128)(2,1)}), bf16[32,8,1536]{2,1,0:T(8,128)(2,1)S(1)}, u32[]{:S(2)}, u32[]{:S(2)}) async-start(bf16[32,8,1536]{2,1,0:T(8,128)(2,1)} %bitcast.100), calls=%async_computation.1 | async-start | bytes 1572864 | tf_op jit(solution)/shard_map/all_to_all | solution.py:39
  51.7 1.5 reshape_squeeze.14
  53.2 2.2 copy.11
  55.4 18.3 %all-to-all-done.1 = bf16[32,8,1536]{2,1,0:T(8,128)(2,1)S(1)} async-done(((bf16[32,8,1536]{2,1,0:T(8,128)(2,1)}), bf16[32,8,1536]{2,1,0:T(8,128)(2,1)S(1)}, u32[]{:S(2)}, u32[]{:S(2)}) %all-to-all-start.1) | async-done | bytes 786464 | tf_op jit(solution)/shard_map/all_to_all | solution.py:39
  73.7 4.9 all-to-all-start.2
  78.6 0.6 reshape_squeeze.15
  79.2 1.0 copy.12
  80.2 20.0 %all-to-all-done.2 = bf16[32,8,1536]{2,1,0:T(8,128)(2,1)S(1)} async-done(((bf16[32,8,1536]{2,1,0:T(8,128)(2,1)}), bf16[32,8,1536]{2,1,0:T(8,128)(2,1)S(1)}, u32[]{:S(2)}, u32[]{:S(2)}) %all-to-all-start.2) | async-done | bytes 786464 | tf_op jit(solution)/shard_map/all_to_all | solution.py:39
  100.2 4.9 all-to-all-start.3
  105.2 3.6 fusion.28
  108.8 5.3 %convolution_add_fusion.2 = f32[512,1536]{1,0:T(8,128)} fusion(f32[512,1536]{1,0:T(8,128)S(1)} %fusion.28, bf16[4,1536,512]{2,1,0:T(8,128)(2,1)} %param.3, s32[]{:T(128)S(6)} %select_n.57, bf16[32,8,1536]{2,1,0:T(8,128)(2,1)} %copy-done), kind=kOutput, calls=%fused_computation.4 | convolution fusion | flops 806223872 | bytes 9437188 | tf_op jit(solution)/shard_map/dot_general | solution.py:16
  114.1 4.7 convolution_add_fusion.1
  118.8 7.8 %all-to-all-done.3 = bf16[32,8,1536]{2,1,0:T(8,128)(2,1)} async-done(((bf16[32,8,1536]{2,1,0:T(8,128)(2,1)}), bf16[32,8,1536]{2,1,0:T(8,128)(2,1)}, u32[]{:S(2)}, u32[]{:S(2)}) %all-to-all-start.3) | async-done | bytes 786464 | tf_op jit(solution)/shard_map/all_to_all | solution.py:39
  126.6 5.3 %fusion = f32[1536,512]{0,1:T(8,128)} fusion(f32[512,1536]{1,0:T(8,128)S(1)} %convolution_add_fusion.1, bf16[4,1536,512]{2,1,0:T(8,128)(2,1)} %param.3, s32[]{:T(128)S(6)} %select_n.57, bf16[32,8,1536]{2,1,0:T(8,128)(2,1)} %all-to-all-done.3), kind=kOutput, calls=%fused_computation.5 | convolution fusion | flops 806223872 | bytes 9437188 | tf_op jit(solution)/shard_map/dot_general | solution.py:16
  132.0 67.8 %all-reduce.3.cloned.1.call-done = f32[1536,512]{0,1:T(8,128)} async-done(((f32[1536,512]{0,1:T(8,128)}), f32[1536,512]{0,1:T(8,128)}) %all-reduce.3.cloned.1.call-update) | async-done | bytes 3145744 | tf_op jit(solution)/shard_map/psum | solution.py:46
  199.8 1.5 constant_dynamic-slice_fusion.3
  201.3 1.6 collective-permute-start
  203.0 35.1 %collective-permute-done = f32[768,512]{0,1:T(8,128)} collective-permute-done((f32[768,512]{0,1:T(8,128)S(1)}, f32[768,512]{0,1:T(8,128)}, u32[]{:S(2)}, u32[]{:S(2)}) %collective-permute-start) | collective-permute-done | bytes 1572896 | tf_op jit(solution)/shard_map/ppermute | solution.py:12
  238.0 2.1 dynamic-slice_add_fusion
  240.2 3.3 collective-permute-start.1
  243.5 18.5 %collective-permute-done.1 = f32[384,512]{0,1:T(8,128)S(1)} collective-permute-done((f32[384,512]{0,1:T(8,128)S(1)}, f32[384,512]{0,1:T(8,128)S(1)}, u32[]{:S(2)}, u32[]{:S(2)}) %collective-permute-start.1) | collective-permute-done | bytes 786464 | tf_op jit(solution)/shard_map/ppermute | solution.py:12
  262.3 1.6 collective-permute-start.2
  263.8 12.2 %collective-permute-done.2 = f32[192,512]{0,1:T(8,128)S(1)} collective-permute-done((f32[192,512]{0,1:T(8,128)S(1)}, f32[192,512]{0,1:T(8,128)S(1)}, u32[]{:S(2)}, u32[]{:S(2)}) %collective-permute-start.2) | collective-permute-done | bytes 393248 | tf_op jit(solution)/shard_map/ppermute | solution.py:12
  276.0 1.2 fusion.66
  277.2 1.6 collective-permute-start.3
  278.8 22.5 %collective-permute-done.3 = f32[512,512]{0,1:T(8,128)S(1)} collective-permute-done((f32[512,512]{0,1:T(8,128)S(1)}, f32[512,512]{0,1:T(8,128)S(1)}, u32[]{:S(2)}, u32[]{:S(2)}) %collective-permute-start.3) | collective-permute-done | bytes 1048608 | tf_op jit(solution)/shard_map/ppermute | solution.py:12
  301.5 3.1 collective-permute-start.4
  304.6 21.5 %collective-permute-done.4 = f32[512,512]{0,1:T(8,128)S(1)} collective-permute-done((f32[512,512]{0,1:T(8,128)S(1)}, f32[512,512]{0,1:T(8,128)S(1)}, u32[]{:S(2)}, u32[]{:S(2)}) %collective-permute-start.4) | collective-permute-done | bytes 1048608 | tf_op jit(solution)/shard_map/ppermute | solution.py:12
  326.4 1.6 collective-permute-start.5
  328.0 1.0 fusion.65
  329.0 19.7 %collective-permute-done.5 = f32[512,512]{0,1:T(8,128)} collective-permute-done((f32[512,512]{0,1:T(8,128)S(1)}, f32[512,512]{0,1:T(8,128)}, u32[]{:S(2)}, u32[]{:S(2)}) %collective-permute-start.5) | collective-permute-done | bytes 1048608 | tf_op jit(solution)/shard_map/ppermute | solution.py:12
  348.7 1.4 add.134
  350.7 11.7 %cholesky.104 = f32[128,128]{1,0:T(8,128)S(1)} custom-call(f32[128,128]{1,0:T(8,128)S(1)} %cholesky.266), custom_call_target="Cholesky" | custom-call | tf_op jit(solution)/shard_map/jit(cholesky)/cholesky | solution.py:57
  362.6 9.8 %custom-call.31 = f32[1,128,128]{1,2,0:T(8,128)S(1)} custom-call(f32[1,128,128]{2,1,0:T(8,128)S(1)} %get-tuple-element.36), custom_call_target="InvertDiagBlocksLowerTriangular" | custom-call | tf_op jit(solution)/shard_map/jit(cholesky)/cholesky | solution.py:57
  373.1 11.7 %cholesky.217 = f32[128,128]{1,0:T(8,128)S(1)} custom-call(f32[128,128]{1,0:T(8,128)S(1)} %cholesky.270), custom_call_target="Cholesky" | custom-call | tf_op jit(solution)/shard_map/jit(cholesky)/cholesky | solution.py:57
  384.9 10.0 %custom-call.32 = f32[1,128,128]{1,2,0:T(8,128)S(1)} custom-call(f32[1,128,128]{2,1,0:T(8,128)S(1)} %get-tuple-element.33), custom_call_target="InvertDiagBlocksLowerTriangular" | custom-call | tf_op jit(solution)/shard_map/jit(cholesky)/cholesky | solution.py:57
  395.5 11.7 %cholesky.238 = f32[128,128]{1,0:T(8,128)S(1)} custom-call(f32[128,128]{1,0:T(8,128)S(1)} %cholesky.275), custom_call_target="Cholesky" | custom-call | tf_op jit(solution)/shard_map/jit(cholesky)/cholesky | solution.py:57
  407.3 9.8 %custom-call.33 = f32[1,128,128]{1,2,0:T(8,128)S(1)} custom-call(f32[1,128,128]{2,1,0:T(8,128)S(1)} %get-tuple-element.30), custom_call_target="InvertDiagBlocksLowerTriangular" | custom-call | tf_op jit(solution)/shard_map/jit(cholesky)/cholesky | solution.py:57
  417.7 11.9 %cholesky.255 = f32[128,128]{1,0:T(8,128)S(1)} custom-call(f32[128,128]{1,0:T(8,128)S(1)} %slice_subtract_fusion.8), custom_call_target="Cholesky" | custom-call | tf_op jit(solution)/shard_map/jit(cholesky)/cholesky | solution.py:57
  429.7 0.7 compare_reduce_fusion.1
  430.4 0.7 compare_reduce_fusion
  431.0 0.6 compare_reduce_fusion.2
  434.3 8.0 %while.1 = (s32[]{:T(128)}, f32[512,512]{1,0:T(8,128)S(1)}, s32[4,2]{0,1:T(2,128)S(1)}, f32[4,128,128]{2,1,0:T(8,128)S(1)}, s32[]{:T(128)}) while((s32[]{:T(128)}, f32[512,512]{1,0:T(8,128)S(1)}, s32[4,2]{0,1:T(2,128)S(1)}, f32[4,128,128]{2,1,0:T(8,128)S(1)}, s32[]{:T(128)}) %tuple.30), condition=%wide.while_cond, body=%wide.while_body.sunk | while | flops 2 | bytes 131189 | solution.py:58
  434.3 0.6 fusion.102
  434.9 1.3 bitcast_dynamic-update-slice_fusion.2
  436.4 0.6 fusion.102
  436.9 1.3 bitcast_dynamic-update-slice_fusion.2
  438.4 0.6 fusion.102
  438.9 1.3 bitcast_dynamic-update-slice_fusion.2
  440.4 0.6 fusion.102
  441.0 1.3 bitcast_dynamic-update-slice_fusion.2
  442.3 39.3 %custom-call.34 = f32[4,128,128]{1,2,0:T(8,128)S(1)} custom-call(f32[4,128,128]{2,1,0:T(8,128)S(1)} %get-tuple-element.12), custom_call_target="InvertDiagBlocksLowerTriangular" | custom-call | tf_op jit(solution)/shard_map/jit(_solve_triangular)/triangular_solve | solution.py:58
  481.6 1.3 fusion.71
  483.3 1.3 fusion.70
  484.9 1.3 fusion.69
  486.7 1.3 fusion.67
  488.0 0.8 fusion.47
  (40 shorter events, 5.2 us)
Async XLA Ops:
  12.2 34.4 %all-to-all-start = ((bf16[32,8,1536]{2,1,0:T(8,128)(2,1)}), bf16[32,8,1536]{2,1,0:T(8,128)(2,1)S(1)}, u32[]{:S(2)}, u32[]{:S(2)}) async-start(bf16[32,8,1536]{2,1,0:T(8,128)(2,1)} %bitcast.101), calls=%async_computation | async-start | bytes 1572864 | tf_op jit(solution)/shard_map/all_to_all | solution.py:39
  46.6 27.0 %copy-start.2 = (bf16[32,8,1536]{2,1,0:T(8,128)(2,1)}, bf16[32,8,1536]{2,1,0:T(8,128)(2,1)S(1)}, u32[]{:S(2)}) copy-start(bf16[32,8,1536]{2,1,0:T(8,128)(2,1)S(1)} %all-to-all-done) | copy-start | bytes 2359300
  46.6 27.0 %all-to-all-start.1 = ((bf16[32,8,1536]{2,1,0:T(8,128)(2,1)}), bf16[32,8,1536]{2,1,0:T(8,128)(2,1)S(1)}, u32[]{:S(2)}, u32[]{:S(2)}) async-start(bf16[32,8,1536]{2,1,0:T(8,128)(2,1)} %bitcast.100), calls=%async_computation.1 | async-start | bytes 1572864 | tf_op jit(solution)/shard_map/all_to_all | solution.py:39
  73.7 26.5 %copy-start = (bf16[32,8,1536]{2,1,0:T(8,128)(2,1)}, bf16[32,8,1536]{2,1,0:T(8,128)(2,1)S(1)}, u32[]{:S(2)}) copy-start(bf16[32,8,1536]{2,1,0:T(8,128)(2,1)S(1)} %all-to-all-done.1) | copy-start | bytes 2359300
  73.7 26.5 %all-to-all-start.2 = ((bf16[32,8,1536]{2,1,0:T(8,128)(2,1)}), bf16[32,8,1536]{2,1,0:T(8,128)(2,1)S(1)}, u32[]{:S(2)}, u32[]{:S(2)}) async-start(bf16[32,8,1536]{2,1,0:T(8,128)(2,1)} %bitcast.8), calls=%async_computation.2 | async-start | bytes 1572864 | tf_op jit(solution)/shard_map/all_to_all | solution.py:39
  100.2 5.0 %copy-start.1 = (bf16[32,8,1536]{2,1,0:T(8,128)(2,1)}, bf16[32,8,1536]{2,1,0:T(8,128)(2,1)S(1)}, u32[]{:S(2)}) copy-start(bf16[32,8,1536]{2,1,0:T(8,128)(2,1)S(1)} %all-to-all-done.2) | copy-start | bytes 2359300
  100.2 26.4 %all-to-all-start.3 = ((bf16[32,8,1536]{2,1,0:T(8,128)(2,1)}), bf16[32,8,1536]{2,1,0:T(8,128)(2,1)}, u32[]{:S(2)}, u32[]{:S(2)}) async-start(bf16[32,8,1536]{2,1,0:T(8,128)(2,1)} %bitcast.11), calls=%async_computation.3 | async-start | bytes 1572864 | tf_op jit(solution)/shard_map/all_to_all | solution.py:39
  105.1 94.7 %all-reduce.3.cloned.1.call-start = ((), (), s32[]{:S(2)}) async-start(), calls=%async_computation.4 | async-start | bytes 6291456 | tf_op jit(solution)/shard_map/psum | solution.py:46
  201.3 36.7 %collective-permute-start = (f32[768,512]{0,1:T(8,128)S(1)}, f32[768,512]{0,1:T(8,128)}, u32[]{:S(2)}, u32[]{:S(2)}) collective-permute-start(f32[768,512]{0,1:T(8,128)S(1)} %constant_dynamic-slice_fusion.3), channel_id=1, source_target_pairs={{0,4},{1,5},{2,6},{3,7},{4,0},{5,1},{6,2},{7,3},{8,12},{9,13},{10,... | collective-permute-start | bytes 4718600 | tf_op jit(solution)/shard_map/ppermute | solution.py:12
  240.2 21.8 %collective-permute-start.1 = (f32[384,512]{0,1:T(8,128)S(1)}, f32[384,512]{0,1:T(8,128)S(1)}, u32[]{:S(2)}, u32[]{:S(2)}) collective-permute-start(f32[384,512]{0,1:T(8,128)S(1)} %constant_dynamic-slice_fusion.2), channel_id=1, source_target_pairs={{0,2},{1,3},{2,0},{3,1},{4,6},{5,7},{6,4},{7,5},{8,10},{9,11},{10,... | collective-permute-start | bytes 2359304 | tf_op jit(solution)/shard_map/ppermute | solution.py:12
  262.3 13.7 %collective-permute-start.2 = (f32[192,512]{0,1:T(8,128)S(1)}, f32[192,512]{0,1:T(8,128)S(1)}, u32[]{:S(2)}, u32[]{:S(2)}) collective-permute-start(f32[192,512]{0,1:T(8,128)S(1)} %constant_dynamic-slice_fusion.1), channel_id=1, source_target_pairs={{0,1},{1,0},{2,3},{3,2},{4,5},{5,4},{6,7},{7,6},{8,9},{9,8},{10,11... | collective-permute-start | bytes 1179656 | tf_op jit(solution)/shard_map/ppermute | solution.py:12
  277.2 24.1 %collective-permute-start.3 = (f32[512,512]{0,1:T(8,128)S(1)}, f32[512,512]{0,1:T(8,128)S(1)}, u32[]{:S(2)}, u32[]{:S(2)}) collective-permute-start(f32[512,512]{0,1:T(8,128)S(1)} %fusion.66), channel_id=1, source_target_pairs={{0,1},{1,0},{2,3},{3,2},{4,5},{5,4},{6,7},{7,6},{8,9},{9,8},{10,11... | collective-permute-start | bytes 3145736 | tf_op jit(solution)/shard_map/ppermute | solution.py:12
  301.5 24.7 %collective-permute-start.4 = (f32[512,512]{0,1:T(8,128)S(1)}, f32[512,512]{0,1:T(8,128)S(1)}, u32[]{:S(2)}, u32[]{:S(2)}) collective-permute-start(f32[512,512]{0,1:T(8,128)S(1)} %add.132), channel_id=1, source_target_pairs={{0,2},{1,3},{2,0},{3,1},{4,6},{5,7},{6,4},{7,5},{8,10},{9,11},{10,... | collective-permute-start | bytes 3145736 | tf_op jit(solution)/shard_map/ppermute | solution.py:12
  326.4 22.3 %collective-permute-start.5 = (f32[512,512]{0,1:T(8,128)S(1)}, f32[512,512]{0,1:T(8,128)}, u32[]{:S(2)}, u32[]{:S(2)}) collective-permute-start(f32[512,512]{0,1:T(8,128)S(1)} %add.133), channel_id=1, source_target_pairs={{0,4},{1,5},{2,6},{3,7},{4,0},{5,1},{6,2},{7,3},{8,12},{9,13},{10,... | collective-permute-start | bytes 3145736 | tf_op jit(solution)/shard_map/ppermute | solution.py:12
Sparse Core Ops, SparseCore 0:
  132.1 67.7 all-reduce.2
where the time goes:
time: 505 us; the launch traced here: 496 us
  waiting for transfers between devices  263 us (52%)
  other arithmetic  124 us (25%)
  starting transfers between devices  39.3 us (8%)
  matrix products  28.3 us (6%)
  local copies, waits for them, and re-layouts  24.7 us (5%)
  between operations  16.6 us (3%)
    ppermute x6, waiting for transfers between devices, swapped(): return lax.ppermute(value, axis, pairs)  129 us
    another operation x14, other arithmetic, on_device(): factor = jnp.linalg.cholesky(gram_small)  78.8 us
    psum x1, waiting for transfers between devices, on_device(): partial_sum = lax.psum(partial_sum, 'dp')  67.8 us
    all_to_all x4, waiting for transfers between devices, on_device(): lax.all_to_all(outgoing, 'seq', split_axis=0, concat_axis=1, tiled=True)  65.4 us
    another operation x3, other arithmetic, on_device(): solved = jax.scipy.linalg.solve_triangular(factor, panel.T, lower=True)  39.4 us
    all_to_all x4, starting transfers between devices, on_device(): lax.all_to_all(outgoing, 'seq', split_axis=0, concat_axis=1, tiled=True)  26.4 us
    dot_general x4, matrix products, contract_rows(): lax.dot_general(left_side, right_side, (((0,), (0,)), ((), ())), preferre...  18.9 us
    ppermute x6, starting transfers between devices, swapped(): return lax.ppermute(value, axis, pairs)  12.8 us
  transfers between devices with their start and end apart: 11, of which 11 were waited for; matrix products, arithmetic and copies ran while one was open for 5% of the time, Pallas kernels for 0%

commit v1 on v0

--- a/solution.py
+++ b/solution.py
@@ -3,7 +3,72 @@
 import jax
 import jax.numpy as jnp
 from jax import lax
+from jax.experimental import pallas as pl
+from jax.experimental.pallas import tpu as pltpu
 from jax.sharding import PartitionSpec as P
+
+HI = lax.Precision.HIGHEST
+
+def diag_inverse(groups):
+    n = len(groups)
+    a = list(groups)
+    sub = lax.broadcasted_iota(jnp.int32, (8, 128), 0)
+    lane = lax.broadcasted_iota(jnp.int32, (8, 128), 1)
+    out = []
+    for s in range(n):
+        c0 = 8 * s
+        r = a[s]
+        b = [jnp.broadcast_to(r[:, c0 + j:c0 + j + 1], (8, 128)) for j in range(8)]
+        pivinv = jnp.zeros((8, 128), jnp.float32)
+        for k in range(8):
+            p = jnp.broadcast_to(b[k][k:k + 1, :], (8, 128))
+            inv = 1.0 / p
+            m = jnp.where(sub > k, b[k] * inv, 0.0)
+            pivinv = jnp.where(sub == k, inv, pivinv)
+            if k < 7:
+                rowk = jnp.broadcast_to(r[k:k + 1, :], (8, 128))
+                rowk = jnp.where(lane == c0 + k, 1.0, rowk)
+                rz = jnp.where((lane == c0 + k) & (sub > k), 0.0, r)
+                r = rz - m * rowk
+                for j in range(k + 1, 8):
+                    b[j] = b[j] - m * jnp.broadcast_to(b[j][k:k + 1, :], (8, 128))
+        rel = lane - c0 - sub
+        rp = jnp.where(rel == 0, 1.0, jnp.where((rel > 0) & (lane < c0 + 8), 0.0, r))
+        if s + 1 < n:
+            un = r * pivinv
+            ut = un.T
+            for t in range(s + 1, n):
+                tt = ut[8 * t:8 * t + 8, :]
+                acc = jnp.where((lane >= c0) & (lane < c0 + 8), 0.0, a[t])
+                for k in range(8):
+                    acc = acc - jnp.broadcast_to(tt[:, k:k + 1], (8, 128)) * jnp.broadcast_to(rp[k:k + 1, :], (8, 128))
+                a[t] = acc
+        out.append(jnp.where(lane < c0 + 8, rp, 0.0) * jnp.sqrt(pivinv))
+    return out
+
+def chol_kernel(g_ref, p_ref, o_ref, a_ref):
+    K = g_ref.shape[0]
+    R = p_ref.shape[0]
+    nb = K // 128
+    a_ref[0:K, :] = g_ref[...]
+    a_ref[K:K + R, :] = p_ref[...]
+    scale = math.sqrt(1536.0)
+    for b in range(nb):
+        lo = 128 * b
+        tiles = [a_ref[lo + 8 * i:lo + 8 * i + 8, lo:lo + 128] for i in range(16)]
+        x = jnp.concatenate(diag_inverse(tiles), axis=0)
+        m = lax.dot_general(a_ref[lo + 128:, lo:lo + 128], x, (((1,), (1,)), ((), ())), precision=HI, preferred_element_type=jnp.float32)
+        nrest = K - lo - 128
+        o_ref[:, lo:lo + 128] = m[nrest:, :] * scale
+        for c in range(b + 1, nb):
+            off = 128 * (c - b - 1)
+            a_ref[128 * c:, 128 * c:128 * c + 128] -= lax.dot_general(m[off:, :], m[off:off + 128, :], (((1,), (1,)), ((), ())), precision=HI, preferred_element_type=jnp.float32)
+
+def chol_solve(g, p):
+    return pl.pallas_call(chol_kernel, out_shape=jax.ShapeDtypeStruct(p.shape, jnp.float32),
+        in_specs=[pl.BlockSpec(memory_space=pltpu.VMEM)] * 2, out_specs=pl.BlockSpec(memory_space=pltpu.VMEM),
+        scratch_shapes=[pltpu.VMEM((g.shape[0] + p.shape[0], g.shape[0]), jnp.float32)],
+        compiler_params=pltpu.CompilerParams(vmem_limit_bytes=32 * 2**20))(g, p)
 
 
 def swapped(value, axis, bit):
@@ -54,9 +119,7 @@
     gram_small = jnp.dot(panel.T, panel, precision=lax.Precision.HIGHEST)
     for bit_pos in range(group_bits):
         gram_small = gram_small + swapped(gram_small, "seq", bit_pos)
-    factor = jnp.linalg.cholesky(gram_small)
-    solved = jax.scipy.linalg.solve_triangular(factor, panel.T, lower=True)
-    return solved.T * math.sqrt(block_width)
+    return chol_solve(gram_small, panel)
 
 
 def solution(mesh):

time: 505 us -> 379 us (0.75); the launches traced: 496 us -> 379 us
  other arithmetic: 124 us -> 2.58 us
  Pallas kernels: 0 us -> 26.3 us
  local copies, waits for them, and re-layouts: 24.7 us -> 16.2 us
  matrix products: 28.3 us -> 20.2 us
    another operation x17 -> x0, other arithmetic: 118 us -> none  [the longest x14 78.8 us: on_device(): factor = jnp.linalg.cholesky(gram_small)]
    pallas_call x0 -> x1, Pallas kernels: none -> 26.3 us  [chol_solve(): pl.pallas_call(chol_kernel, out_shape=jax.ShapeDtypeStruct(p.shape, jnp.f...]
    another operation x13 -> x0, matrix products: 8.21 us -> none  [the longest x7 6.34 us: on_device(): solved = jax.scipy.linalg.solve_triangular(factor, panel.T, lower=True)]
    another operation x17 -> x0, local copies, waits for them, and re-layouts: 8.1 us -> none
  transfers between devices with their start and end apart: 11 -> 11, of which waited for: 11 -> 11; matrix products, arithmetic and copies ran while one was open for 5% -> 6% of each run, Pallas kernels for 0% -> 0%
where the time goes in v1:
time: 379 us
  waiting for transfers between devices  260 us (69%)
  starting transfers between devices  39.5 us (10%)
  Pallas kernels  26.3 us (7%)
  matrix products  20.2 us (5%)
  local copies, waits for them, and re-layouts  16.2 us (4%)
  between operations  13.6 us (4%)
    ppermute x6, waiting for transfers between devices, swapped(): return lax.ppermute(value, axis, pairs)  128 us
    psum x1, waiting for transfers between devices, on_device(): partial_sum = lax.psum(partial_sum, 'dp')  67.8 us
    all_to_all x4, waiting for transfers between devices, on_device(): lax.all_to_all(outgoing, 'seq', split_axis=0, concat_axis=1, tiled=True)  65.1 us
    all_to_all x4, starting transfers between devices, on_device(): lax.all_to_all(outgoing, 'seq', split_axis=0, concat_axis=1, tiled=True)  26.4 us
    pallas_call x1, Pallas kernels, chol_solve(): pl.pallas_call(chol_kernel, out_shape=jax.ShapeDtypeStruct(p.shape, jnp.f...  26.3 us
    dot_general x4, matrix products, contract_rows(): lax.dot_general(left_side, right_side, (((0,), (0,)), ((), ())), preferre...  19.1 us
    ppermute x6, starting transfers between devices, swapped(): return lax.ppermute(value, axis, pairs)  12.8 us
  transfers between devices with their start and end apart: 11, of which 11 were waited for; matrix products, arithmetic and copies ran while one was open for 6% of the time, Pallas kernels for 0%

profile of v1, /device:TPU:6, one launch (start us, length us, event | category | flops | bytes accessed | tf_op | source)
XLA Modules:
  0.0 378.7 jit_solution(10929903845718168604)
XLA Ops:
  6.5 2.0 fusion.54
  8.6 1.5 reshape_squeeze.12
  10.1 2.2 copy.11
  12.2 11.5 %all-to-all-start = ((bf16[32,8,1536]{2,1,0:T(8,128)(2,1)}), bf16[32,8,1536]{2,1,0:T(8,128)(2,1)S(1)}, u32[]{:S(2)}, u32[]{:S(2)}) async-start(bf16[32,8,1536]{2,1,0:T(8,128)(2,1)} %bitcast.54), calls=%async_computation | async-start | bytes 1572864 | tf_op jit(solution)/shard_map/all_to_all | solution.py:104
  23.7 1.5 reshape_squeeze.13
  25.2 2.2 copy.12
  27.4 19.3 %all-to-all-done = bf16[32,8,1536]{2,1,0:T(8,128)(2,1)S(1)} async-done(((bf16[32,8,1536]{2,1,0:T(8,128)(2,1)}), bf16[32,8,1536]{2,1,0:T(8,128)(2,1)S(1)}, u32[]{:S(2)}, u32[]{:S(2)}) %all-to-all-start) | async-done | bytes 786464 | tf_op jit(solution)/shard_map/all_to_all | solution.py:104
  46.6 0.0 copy-start.2
  46.7 5.1 %all-to-all-start.1 = ((bf16[32,8,1536]{2,1,0:T(8,128)(2,1)}), bf16[32,8,1536]{2,1,0:T(8,128)(2,1)S(1)}, u32[]{:S(2)}, u32[]{:S(2)}) async-start(bf16[32,8,1536]{2,1,0:T(8,128)(2,1)} %bitcast.53), calls=%async_computation.1 | async-start | bytes 1572864 | tf_op jit(solution)/shard_map/all_to_all | solution.py:104
  51.7 1.5 reshape_squeeze.14
  53.2 2.1 copy.15
  55.4 18.3 %all-to-all-done.1 = bf16[32,8,1536]{2,1,0:T(8,128)(2,1)S(1)} async-done(((bf16[32,8,1536]{2,1,0:T(8,128)(2,1)}), bf16[32,8,1536]{2,1,0:T(8,128)(2,1)S(1)}, u32[]{:S(2)}, u32[]{:S(2)}) %all-to-all-start.1) | async-done | bytes 786464 | tf_op jit(solution)/shard_map/all_to_all | solution.py:104
  73.7 0.0 copy-start
  73.7 0.0 copy-done.2
  73.7 4.9 %all-to-all-start.2 = ((bf16[32,8,1536]{2,1,0:T(8,128)(2,1)}), bf16[32,8,1536]{2,1,0:T(8,128)(2,1)S(1)}, u32[]{:S(2)}, u32[]{:S(2)}) async-start(bf16[32,8,1536]{2,1,0:T(8,128)(2,1)} %bitcast.8), calls=%async_computation.2 | async-start | bytes 1572864 | tf_op jit(solution)/shard_map/all_to_all | solution.py:104
  78.6 0.6 reshape_squeeze.15
  79.2 1.0 copy.17
  80.2 20.0 %all-to-all-done.2 = bf16[32,8,1536]{2,1,0:T(8,128)(2,1)S(1)} async-done(((bf16[32,8,1536]{2,1,0:T(8,128)(2,1)}), bf16[32,8,1536]{2,1,0:T(8,128)(2,1)S(1)}, u32[]{:S(2)}, u32[]{:S(2)}) %all-to-all-start.2) | async-done | bytes 786464 | tf_op jit(solution)/shard_map/all_to_all | solution.py:104
  100.2 0.0 copy-start.1
  100.2 0.0 copy-done
  100.2 4.9 %all-to-all-start.3 = ((bf16[32,8,1536]{2,1,0:T(8,128)(2,1)}), bf16[32,8,1536]{2,1,0:T(8,128)(2,1)}, u32[]{:S(2)}, u32[]{:S(2)}) async-start(bf16[32,8,1536]{2,1,0:T(8,128)(2,1)} %bitcast.11), calls=%async_computation.3 | async-start | bytes 1572864 | tf_op jit(solution)/shard_map/all_to_all | solution.py:104
  105.1 0.2 all-reduce.2.cloned.1.call-start
  105.4 0.0 copy-done.1
  105.4 3.7 fusion.28
  109.1 5.4 %convolution_add_fusion.2 = f32[512,1536]{0,1:T(8,128)} fusion(f32[512,1536]{0,1:T(8,128)S(1)} %fusion.28, bf16[4,1536,512]{2,1,0:T(8,128)(2,1)} %param.3, s32[]{:T(128)S(6)} %select_n.53, bf16[32,8,1536]{2,1,0:T(8,128)(2,1)} %copy-done), kind=kOutput, calls=%fused_computation.2 | convolution fusion | flops 806223872 | bytes 9437188 | tf_op jit(solution)/shard_map/dot_general | solution.py:81
  114.4 4.7 %convolution_add_fusion.1 = f32[512,1536]{0,1:T(8,128)S(1)} fusion(f32[512,1536]{0,1:T(8,128)} %convolution_add_fusion.2, bf16[4,1536,512]{2,1,0:T(8,128)(2,1)} %param.3, s32[]{:T(128)S(6)} %select_n.53, bf16[32,8,1536]{2,1,0:T(8,128)(2,1)} %copy-done.1), kind=kOutput, calls=%fused_computation.1 | convolution fusion | flops 806223872 | bytes 9437188 | tf_op jit(solution)/shard_map/dot_general | solution.py:81
  119.1 7.5 %all-to-all-done.3 = bf16[32,8,1536]{2,1,0:T(8,128)(2,1)} async-done(((bf16[32,8,1536]{2,1,0:T(8,128)(2,1)}), bf16[32,8,1536]{2,1,0:T(8,128)(2,1)}, u32[]{:S(2)}, u32[]{:S(2)}) %all-to-all-start.3) | async-done | bytes 786464 | tf_op jit(solution)/shard_map/all_to_all | solution.py:104
  126.6 5.3 %fusion = f32[1536,512]{1,0:T(8,128)} fusion(f32[512,1536]{0,1:T(8,128)S(1)} %convolution_add_fusion.1, bf16[4,1536,512]{2,1,0:T(8,128)(2,1)} %param.3, s32[]{:T(128)S(6)} %select_n.53, bf16[32,8,1536]{2,1,0:T(8,128)(2,1)} %all-to-all-done.3), kind=kOutput, calls=%fused_computation.3 | convolution fusion | flops 806223872 | bytes 9437188 | tf_op jit(solution)/shard_map/dot_general | solution.py:81
  131.9 0.0 all-reduce.2.cloned.1.call-update
  132.0 67.8 %all-reduce.2.cloned.1.call-done = f32[1536,512]{1,0:T(8,128)} async-done(((f32[1536,512]{1,0:T(8,128)}), f32[1536,512]{1,0:T(8,128)}) %all-reduce.2.cloned.1.call-update) | async-done | bytes 3145744 | tf_op jit(solution)/shard_map/psum | solution.py:111
  199.9 1.5 constant_dynamic-slice_fusion.2
  201.4 1.6 collective-permute-start
  203.0 35.0 %collective-permute-done = f32[768,512]{1,0:T(8,128)S(1)} collective-permute-done((f32[768,512]{1,0:T(8,128)S(1)}, f32[768,512]{1,0:T(8,128)S(1)}, u32[]{:S(2)}, u32[]{:S(2)}) %collective-permute-start) | collective-permute-done | bytes 1572896 | tf_op jit(solution)/shard_map/ppermute | solution.py:77
  238.0 1.8 dynamic-slice_add_fusion
  239.7 0.1 constant_dynamic-slice_fusion.1
  239.8 3.1 collective-permute-start.1
  242.9 18.5 %collective-permute-done.1 = f32[384,512]{1,0:T(8,128)S(1)} collective-permute-done((f32[384,512]{1,0:T(8,128)S(1)}, f32[384,512]{1,0:T(8,128)S(1)}, u32[]{:S(2)}, u32[]{:S(2)}) %collective-permute-start.1) | collective-permute-done | bytes 786464 | tf_op jit(solution)/shard_map/ppermute | solution.py:77
  261.4 0.1 dynamic-slice_add_fusion.1
  261.6 1.6 collective-permute-start.2
  263.2 9.3 %collective-permute-done.2 = f32[192,512]{1,0:T(8,128)S(1)} collective-permute-done((f32[192,512]{1,0:T(8,128)S(1)}, f32[192,512]{1,0:T(8,128)S(1)}, u32[]{:S(2)}, u32[]{:S(2)}) %collective-permute-start.2) | collective-permute-done | bytes 393248 | tf_op jit(solution)/shard_map/ppermute | solution.py:77
  272.5 0.1 add_multiply_fusion.p_ref
  272.6 1.1 fusion.55
  273.7 1.6 collective-permute-start.3
  275.3 22.5 %collective-permute-done.3 = f32[512,512]{1,0:T(8,128)S(1)} collective-permute-done((f32[512,512]{1,0:T(8,128)S(1)}, f32[512,512]{1,0:T(8,128)S(1)}, u32[]{:S(2)}, u32[]{:S(2)}) %collective-permute-start.3) | collective-permute-done | bytes 1048608 | tf_op jit(solution)/shard_map/ppermute | solution.py:77
  297.8 0.2 add.91
  298.0 3.1 collective-permute-start.4
  301.1 21.6 %collective-permute-done.4 = f32[512,512]{1,0:T(8,128)S(1)} collective-permute-done((f32[512,512]{1,0:T(8,128)S(1)}, f32[512,512]{1,0:T(8,128)S(1)}, u32[]{:S(2)}, u32[]{:S(2)}) %collective-permute-start.4) | collective-permute-done | bytes 1048608 | tf_op jit(solution)/shard_map/ppermute | solution.py:77
  322.7 0.2 add.92
  322.9 1.9 collective-permute-start.5
  324.8 20.6 %collective-permute-done.5 = f32[512,512]{1,0:T(8,128)S(1)} collective-permute-done((f32[512,512]{1,0:T(8,128)S(1)}, f32[512,512]{1,0:T(8,128)S(1)}, u32[]{:S(2)}, u32[]{:S(2)}) %collective-permute-start.5) | collective-permute-done | bytes 1048608 | tf_op jit(solution)/shard_map/ppermute | solution.py:77
  345.4 0.2 add.93.g_ref
  345.6 26.3 %shard_map.28 = f32[192,512]{1,0:T(8,128)} custom-call(f32[512,512]{1,0:T(8,128)S(1)} %add.93.g_ref, f32[192,512]{1,0:T(8,128)S(1)} %add_multiply_fusion.p_ref), custom_call_target="tpu_custom_call" | custom-call | tf_op jit(solution)/shard_map/pallas_call | solution.py:68
  (1 shorter events, 0.0 us)
Async XLA Ops:
  12.2 34.4 %all-to-all-start = ((bf16[32,8,1536]{2,1,0:T(8,128)(2,1)}), bf16[32,8,1536]{2,1,0:T(8,128)(2,1)S(1)}, u32[]{:S(2)}, u32[]{:S(2)}) async-start(bf16[32,8,1536]{2,1,0:T(8,128)(2,1)} %bitcast.54), calls=%async_computation | async-start | bytes 1572864 | tf_op jit(solution)/shard_map/all_to_all | solution.py:104
  46.6 27.0 %copy-start.2 = (bf16[32,8,1536]{2,1,0:T(8,128)(2,1)}, bf16[32,8,1536]{2,1,0:T(8,128)(2,1)S(1)}, u32[]{:S(2)}) copy-start(bf16[32,8,1536]{2,1,0:T(8,128)(2,1)S(1)} %all-to-all-done) | copy-start | bytes 2359300
  46.7 27.0 %all-to-all-start.1 = ((bf16[32,8,1536]{2,1,0:T(8,128)(2,1)}), bf16[32,8,1536]{2,1,0:T(8,128)(2,1)S(1)}, u32[]{:S(2)}, u32[]{:S(2)}) async-start(bf16[32,8,1536]{2,1,0:T(8,128)(2,1)} %bitcast.53), calls=%async_computation.1 | async-start | bytes 1572864 | tf_op jit(solution)/shard_map/all_to_all | solution.py:104
  73.7 26.5 %copy-start = (bf16[32,8,1536]{2,1,0:T(8,128)(2,1)}, bf16[32,8,1536]{2,1,0:T(8,128)(2,1)S(1)}, u32[]{:S(2)}) copy-start(bf16[32,8,1536]{2,1,0:T(8,128)(2,1)S(1)} %all-to-all-done.1) | copy-start | bytes 2359300
  73.7 26.5 %all-to-all-start.2 = ((bf16[32,8,1536]{2,1,0:T(8,128)(2,1)}), bf16[32,8,1536]{2,1,0:T(8,128)(2,1)S(1)}, u32[]{:S(2)}, u32[]{:S(2)}) async-start(bf16[32,8,1536]{2,1,0:T(8,128)(2,1)} %bitcast.8), calls=%async_computation.2 | async-start | bytes 1572864 | tf_op jit(solution)/shard_map/all_to_all | solution.py:104
  100.2 5.2 %copy-start.1 = (bf16[32,8,1536]{2,1,0:T(8,128)(2,1)}, bf16[32,8,1536]{2,1,0:T(8,128)(2,1)S(1)}, u32[]{:S(2)}) copy-start(bf16[32,8,1536]{2,1,0:T(8,128)(2,1)S(1)} %all-to-all-done.2) | copy-start | bytes 2359300
  100.2 26.4 %all-to-all-start.3 = ((bf16[32,8,1536]{2,1,0:T(8,128)(2,1)}), bf16[32,8,1536]{2,1,0:T(8,128)(2,1)}, u32[]{:S(2)}, u32[]{:S(2)}) async-start(bf16[32,8,1536]{2,1,0:T(8,128)(2,1)} %bitcast.11), calls=%async_computation.3 | async-start | bytes 1572864 | tf_op jit(solution)/shard_map/all_to_all | solution.py:104
  105.1 94.8 %all-reduce.2.cloned.1.call-start = ((), (), s32[]{:S(2)}) async-start(), calls=%async_computation.4 | async-start | bytes 6291456 | tf_op jit(solution)/shard_map/psum | solution.py:111
  201.4 36.6 %collective-permute-start = (f32[768,512]{1,0:T(8,128)S(1)}, f32[768,512]{1,0:T(8,128)S(1)}, u32[]{:S(2)}, u32[]{:S(2)}) collective-permute-start(f32[768,512]{1,0:T(8,128)S(1)} %constant_dynamic-slice_fusion.2), channel_id=1, source_target_pairs={{0,4},{1,5},{2,6},{3,7},{4,0},{5,1},{6,2},{7,3},{8,12},{9,13},{10,... | collective-permute-start | bytes 4718600 | tf_op jit(solution)/shard_map/ppermute | solution.py:77
  239.8 21.6 %collective-permute-start.1 = (f32[384,512]{1,0:T(8,128)S(1)}, f32[384,512]{1,0:T(8,128)S(1)}, u32[]{:S(2)}, u32[]{:S(2)}) collective-permute-start(f32[384,512]{1,0:T(8,128)S(1)} %constant_dynamic-slice_fusion.1), channel_id=1, source_target_pairs={{0,2},{1,3},{2,0},{3,1},{4,6},{5,7},{6,4},{7,5},{8,10},{9,11},{10,... | collective-permute-start | bytes 2359304 | tf_op jit(solution)/shard_map/ppermute | solution.py:77
  261.6 10.9 %collective-permute-start.2 = (f32[192,512]{1,0:T(8,128)S(1)}, f32[192,512]{1,0:T(8,128)S(1)}, u32[]{:S(2)}, u32[]{:S(2)}) collective-permute-start(f32[192,512]{1,0:T(8,128)S(1)} %constant_dynamic-slice_fusion), channel_id=1, source_target_pairs={{0,1},{1,0},{2,3},{3,2},{4,5},{5,4},{6,7},{7,6},{8,9},{9,8},{10,11... | collective-permute-start | bytes 1179656 | tf_op jit(solution)/shard_map/ppermute | solution.py:77
  273.7 24.1 %collective-permute-start.3 = (f32[512,512]{1,0:T(8,128)S(1)}, f32[512,512]{1,0:T(8,128)S(1)}, u32[]{:S(2)}, u32[]{:S(2)}) collective-permute-start(f32[512,512]{1,0:T(8,128)S(1)} %fusion.55), channel_id=1, source_target_pairs={{0,1},{1,0},{2,3},{3,2},{4,5},{5,4},{6,7},{7,6},{8,9},{9,8},{10,11... | collective-permute-start | bytes 3145736 | tf_op jit(solution)/shard_map/ppermute | solution.py:77
  298.0 24.7 %collective-permute-start.4 = (f32[512,512]{1,0:T(8,128)S(1)}, f32[512,512]{1,0:T(8,128)S(1)}, u32[]{:S(2)}, u32[]{:S(2)}) collective-permute-start(f32[512,512]{1,0:T(8,128)S(1)} %add.91), channel_id=1, source_target_pairs={{0,2},{1,3},{2,0},{3,1},{4,6},{5,7},{6,4},{7,5},{8,10},{9,11},{10,... | collective-permute-start | bytes 3145736 | tf_op jit(solution)/shard_map/ppermute | solution.py:77
  322.9 22.5 %collective-permute-start.5 = (f32[512,512]{1,0:T(8,128)S(1)}, f32[512,512]{1,0:T(8,128)S(1)}, u32[]{:S(2)}, u32[]{:S(2)}) collective-permute-start(f32[512,512]{1,0:T(8,128)S(1)} %add.92), channel_id=1, source_target_pairs={{0,4},{1,5},{2,6},{3,7},{4,0},{5,1},{6,2},{7,3},{8,12},{9,13},{10,... | collective-permute-start | bytes 3145736 | tf_op jit(solution)/shard_map/ppermute | solution.py:77
Sparse Core Ops, SparseCore 0:
  132.1 67.7 all-reduce.1

commit v2 on v1

v2 whole, which is shorter than its diff:
```python
import math

import jax
import jax.numpy as jnp
from jax import lax
from jax.experimental import pallas as pl
from jax.experimental.pallas import tpu as pltpu
from jax.sharding import PartitionSpec as P

F32, BF16 = jnp.float32, jnp.bfloat16
NX, NC, NZ, NY = 4, 2, 8, 4
HI = lax.Precision.HIGHEST
STAGES = (("z", "y", "x"), ("y", "x", "z"), ("x", "z", "y"))
SIZE = {"x": NX, "y": NY, "z": NZ}


class Copies:
    def __init__(self, send_sems, recv_sems):
        self.send_sems, self.recv_sems, self.count, self.made = send_sems, recv_sems, 0, []

    def send(self, src, dst, device):
        n = self.count
        self.count += 1
        copy = pltpu.make_async_remote_copy(
            src_ref=src, dst_ref=dst, send_sem=self.send_sems.at[n], recv_sem=self.recv_sems.at[n],
            device_id=device, device_id_type=pl.DeviceIdType.MESH,
        )
        copy.start()
        self.made.append(copy)
        return copy


def ring(copies, n, me, piece, half, to, up_s, up_r, dn_s, dn_r, up_h, dn_h, up_hr, dn_hr):
    steps = n // 2
    far = piece(lax.rem(me + steps, n))
    up_h[...] = far[:half].astype(BF16)
    dn_h[...] = far[half:].astype(BF16)
    up = copies.send(up_h, up_hr, to(lax.rem(me + 1, n)))
    dn = copies.send(dn_h, dn_hr, to(lax.rem(me + n - 1, n)))
    yield
    for i in range(1, steps):
        d = steps - i
        mine = piece(lax.rem(me + d, n))
        up.wait_recv()
        if i == 1:
            up_s[0, :half] = (mine[:half] + up_hr[...].astype(F32)).astype(BF16)
            up_s[0, half:] = mine[half:].astype(BF16)
        else:
            up_s[i - 1] = (mine + up_r[i - 2].astype(F32)).astype(BF16)
        up = copies.send(up_s.at[i - 1], up_r.at[i - 1], to(lax.rem(me + 1, n)))
        mine = piece(lax.rem(me + n - d, n))
        dn.wait_recv()
        if i == 1:
            dn_s[0, half:] = (mine[half:] + dn_hr[...].astype(F32)).astype(BF16)
            dn_s[0, :half] = mine[:half].astype(BF16)
        else:
            dn_s[i - 1] = (mine + dn_r[i - 2].astype(F32)).astype(BF16)
        dn = copies.send(dn_s.at[i - 1], dn_r.at[i - 1], to(lax.rem(me + n - 1, n)))
        yield
    up.wait_recv()
    dn.wait_recv()
    return piece(me) + up_r[steps - 2].astype(F32) + dn_r[steps - 2].astype(F32)


def direct(copies, n, me, piece, to, bufs, bufr):
    sent = []
    for d in range(1, n):
        bufs[d - 1] = piece(lax.rem(me + d, n)).astype(bufs.dtype)
        sent.append(copies.send(bufs.at[d - 1], bufr.at[d - 1], to(lax.rem(me + d, n))))
    yield
    total = piece(me)
    for d in range(1, n):
        sent[d - 1].wait_recv()
        total = total + bufr[d - 1].astype(F32)
    return total


def kernel(act, basis, p_out, g_out, *scratch):
    (a_v, b_v, proj, pan, p_v, g_v, gs, gsum, gr, load_sems, send_sems, recv_sems, out_sems,
     *bufs) = scratch
    bufs = list(bufs)
    dp, seq = lax.axis_index("dp"), lax.axis_index("seq")
    x, c, z, y = dp // 2, lax.rem(dp, 2), seq // NY, lax.rem(seq, NY)
    zz = lax.rem(z, 2)
    me = {"x": x, "y": y, "z": z}

    def dev(x_=None, c_=None, z_=None, y_=None):
        x_, c_, z_, y_ = (x if x_ is None else x_, c if c_ is None else c_,
                          z if z_ is None else z_, y if y_ is None else y_)
        return (x_ * NC + c_, z_ * NY + y_)

    order = [lax.rem(z // 2 + o, 4) for o in (2, 1, 3, 0)]
    own_loads, b_loads = [], []
    for i, j in enumerate(order):
        cols = pl.ds(pl.multiple_of(j * 1536, 1536), 1536)
        b_loads.append(pltpu.make_async_copy(
            basis.at[j, :, pl.ds(pl.multiple_of(c * 256, 256), 256)], b_v.at[i], load_sems.at[i]))
        own_loads.append(pltpu.make_async_copy(act.at[:, :, cols], a_v.at[i, 0], load_sems.at[4 + i]))
        own_loads[i].start()
        b_loads[i].start()

    peers = [dev(c_=1 - c)]
    for d in range(1, NX):
        peers += [dev(x_=lax.rem(x + d, NX)), dev(x_=lax.rem(x + d, NX), c_=1 - c)]
    for d in range(1, NY):
        peers += [dev(y_=lax.rem(y + d, NY)), dev(z_=z + 1 - 2 * zz, y_=lax.rem(y + d, NY))]
    for d in range(1, NZ):
        peers.append(dev(z_=lax.rem(z + d, NZ)))
    barrier = pltpu.get_barrier_semaphore()
    for peer in peers:
        pl.semaphore_signal(barrier, inc=1, device_id=peer, device_id_type=pl.DeviceIdType.MESH)
    pl.semaphore_wait(barrier, len(peers))

    copies = Copies(send_sems, recv_sems)
    exchanged = []
    for i, j in enumerate(order):
        cols = pl.ds(pl.multiple_of(j * 1536, 1536), 1536)
        exchanged.append(copies.send(act.at[:, :, cols], a_v.at[i, 1], dev(c_=1 - c)))

    shares = [8 + 1 + 2 + 1 + 2] * 3
    pools = []
    for share in shares:
        pools.append(bufs[:share])
        bufs = bufs[share:]

    def stream_with(t, pool):
        axes = STAGES[t]
        pool = list(pool)
        cur = pan.at[t]
        left = ["z", "y", "x"]
        for stage, axis in enumerate(axes):
            n = SIZE[axis]
            pos = left.index(axis)
            left.pop(pos)

            def piece(dest, cur=cur, pos=pos):
                return cur[(slice(None),) * pos + (dest,)]

            def to(dest, axis=axis):
                return dev(**{axis + "_": dest})

            if stage == 0:
                taken, pool = pool[:8], pool[8:]
                total = yield from ring(copies, n, me[axis], piece, taken[4].shape[0], to, *taken)
            else:
                taken, pool = pool[:2], pool[2:]
                total = yield from direct(copies, n, me[axis], piece, to, *taken)
            if stage < 2:
                cur = pool.pop(0)
                cur[...] = total
            else:
                p_v[c, x, 16 * t:16 * t + 16, :] = total * (1.0 / 65536.0)

    gens = [stream_with(t, pools[t]) for t in range(3)]

    def compute(i):
        j = order[i]
        b_loads[i].wait()
        own_loads[i].wait()
        proj[0:256, :] = jnp.dot(a_v[i, 0].reshape(256, 1536), b_v[i], preferred_element_type=F32).astype(BF16)
        exchanged[i].wait_recv()
        proj[256:512, :] = jnp.dot(a_v[i, 1].reshape(256, 1536), b_v[i], preferred_element_type=F32).astype(BF16)
        for k in range(4):
            lhs = a_v[i, :, :, :, 384 * k:384 * k + 384].reshape(512, 384)
            r = lax.dot_general(lhs, proj[...], (((0,), (0,)), ((), ())), preferred_element_type=F32)
            r = r.reshape(2, 4, 3, 16, 256)
            for t in range(3):
                pan[t, 2 * j + k // 2, 2 * (k % 2):2 * (k % 2) + 2] = r[:, :, t]

    compute(0)
    next(gens[0])
    for i in range(1, 4):
        compute(i)
    live = [1, 2, 0]
    while live:
        for t in list(live):
            try:
                next(gens[t])
            except StopIteration:
                live.remove(t)

    sent = []
    for d in range(1, 8):
        sent.append(copies.send(p_v.at[c, x], p_v.at[c, x],
                                dev(x_=lax.rem(x + d // 2, NX), c_=c if d % 2 == 0 else 1 - c)))
    for copy in sent:
        copy.wait_recv()

    blk = p_v[x // 2, :, :, pl.ds(pl.multiple_of(lax.rem(x, 2) * 128, 128), 128)].reshape(192, 128)
    for h in range(2):
        gs[:, :, 256 * h:256 * h + 256] = lax.dot_general(
            blk, p_v[h].reshape(192, 256), (((0,), (0,)), ((), ())), precision=HI,
            preferred_element_type=F32).reshape(16, 8, 256)
    p_me = zz * NY + y
    sent = []
    for d in range(1, 8):
        q = lax.rem(p_me + d, 8)
        sent.append(copies.send(gs.at[8 * c + q], gr.at[d - 1], dev(z_=z - zz + q // NY, y_=lax.rem(q, NY))))
    total = gs[8 * c + p_me]
    for d in range(1, 8):
        sent[d - 1].wait_recv()
        total = total + gr[d - 1]
    g_v[c, x, p_me] = total
    sent = []
    for d in range(1, 8):
        q = lax.rem(p_me + d, 8)
        sent.append(copies.send(g_v.at[c, x, p_me], g_v.at[c, x, p_me], dev(z_=z - zz + q // NY, y_=lax.rem(q, NY))))
    for copy in sent:
        copy.wait_recv()
    sent = []
    for d in range(1, NX):
        sent.append(copies.send(g_v.at[c, x], g_v.at[c, x], dev(x_=lax.rem(x + d, NX))))
    for copy in sent:
        copy.wait_recv()
    last = copies.send(g_v.at[c], g_v.at[c], dev(c_=1 - c))
    p_done = pltpu.make_async_copy(p_v, p_out, out_sems.at[0])
    p_done.start()
    last.wait_recv()
    g_done = pltpu.make_async_copy(g_v, g_out, out_sems.at[1])
    g_done.start()
    for copy in copies.made:
        copy.wait_send()
    p_done.wait()
    g_done.wait()


def panel_and_gram(act, basis):
    piece = {"x": (NZ, NY), "y": (NZ, NX), "z": (NY, NX)}
    tile = (16, 256)
    bufs = []
    for axes in STAGES:
        left = ["z", "y", "x"]
        for stage, axis in enumerate(axes):
            left.remove(axis)
            n = SIZE[axis]
            shape = tuple(SIZE[a] for a in left) + tile
            if stage == 0:
                half = (shape[0] // 2,) + shape[1:]
                full = (n // 2 - 1,) + shape
                bufs += [pltpu.VMEM(full, BF16)] * 4 + [pltpu.VMEM(half, BF16)] * 4
            else:
                bufs += [pltpu.VMEM((n - 1,) + shape, BF16 if stage == 1 else F32)] * 2
            if stage < 2:
                bufs.append(pltpu.VMEM(shape, F32))
    return pl.pallas_call(
        kernel,
        out_shape=(jax.ShapeDtypeStruct((NC, NX, 48, 256), F32),
                   jax.ShapeDtypeStruct((NC, NX, 8, 8, 512), F32)),
        in_specs=[pl.BlockSpec(memory_space=pl.ANY)] * 2,
        out_specs=[pl.BlockSpec(memory_space=pl.ANY)] * 2,
        scratch_shapes=[
            pltpu.VMEM((4, 2, 4, 64, 1536), BF16),
            pltpu.VMEM((4, 1536, 256), BF16),
            pltpu.VMEM((512, 256), BF16),
            pltpu.VMEM((3, NZ, NY, NX, 16, 256), F32),
            pltpu.VMEM((NC, NX, 48, 256), F32),
            pltpu.VMEM((NC, NX, 8, 8, 512), F32),
            pltpu.VMEM((16, 8, 512), F32),
            pltpu.VMEM((8, 512), F32),
            pltpu.VMEM((7, 8, 512), F32),
            pltpu.SemaphoreType.DMA((8,)),
            pltpu.SemaphoreType.DMA((96,)),
            pltpu.SemaphoreType.DMA((96,)),
            pltpu.SemaphoreType.DMA((2,)),
        ] + bufs,
        compiler_params=pltpu.CompilerParams(
            collective_id=1, has_side_effects=True, vmem_limit_bytes=56 * 2**20),
    )(act, basis)


def diag_inverse(groups):
    n = len(groups)
    a = list(groups)
    sub = lax.broadcasted_iota(jnp.int32, (8, 128), 0)
    lane = lax.broadcasted_iota(jnp.int32, (8, 128), 1)
    out = []
    for s in range(n):
        c0 = 8 * s
        r = a[s]
        b = [jnp.broadcast_to(r[:, c0 + j:c0 + j + 1], (8, 128)) for j in range(8)]
        pivinv = jnp.zeros((8, 128), jnp.float32)
        for k in range(8):
            p = jnp.broadcast_to(b[k][k:k + 1, :], (8, 128))
            inv = 1.0 / p
            m = jnp.where(sub > k, b[k] * inv, 0.0)
            pivinv = jnp.where(sub == k, inv, pivinv)
            if k < 7:
                rowk = jnp.broadcast_to(r[k:k + 1, :], (8, 128))
                rowk = jnp.where(lane == c0 + k, 1.0, rowk)
                rz = jnp.where((lane == c0 + k) & (sub > k), 0.0, r)
                r = rz - m * rowk
                for j in range(k + 1, 8):
                    b[j] = b[j] - m * jnp.broadcast_to(b[j][k:k + 1, :], (8, 128))
        rel = lane - c0 - sub
        rp = jnp.where(rel == 0, 1.0, jnp.where((rel > 0) & (lane < c0 + 8), 0.0, r))
        if s + 1 < n:
            un = r * pivinv
            ut = un.T
            for t in range(s + 1, n):
                tt = ut[8 * t:8 * t + 8, :]
                acc = jnp.where((lane >= c0) & (lane < c0 + 8), 0.0, a[t])
                for k in range(8):
                    acc = acc - jnp.broadcast_to(tt[:, k:k + 1], (8, 128)) * jnp.broadcast_to(rp[k:k + 1, :], (8, 128))
                a[t] = acc
        out.append(jnp.where(lane < c0 + 8, rp, 0.0) * jnp.sqrt(pivinv))
    return out

def chol_kernel(g_ref, p_ref, o_ref, a_ref):
    K, R = 512, 192
    nb = K // 128
    for c in range(NC):
        for x in range(NX):
            a_ref[128 * x + 64 * c:128 * x + 64 * c + 64, :] = g_ref[c, x].reshape(64, K)
            a_ref[K + 48 * x:K + 48 * x + 48, 256 * c:256 * c + 256] = p_ref[c, x]
    scale = math.sqrt(1536.0)
    for b in range(nb):
        lo = 128 * b
        tiles = [a_ref[lo + 8 * i:lo + 8 * i + 8, lo:lo + 128] for i in range(16)]
        x = jnp.concatenate(diag_inverse(tiles), axis=0)
        m = lax.dot_general(a_ref[lo + 128:, lo:lo + 128], x, (((1,), (1,)), ((), ())),
                            precision=HI, preferred_element_type=F32)
        nrest = K - lo - 128
        o_ref[:, lo:lo + 128] = m[nrest:, :] * scale
        for c in range(b + 1, nb):
            off = 128 * (c - b - 1)
            a_ref[128 * c:, 128 * c:128 * c + 128] -= lax.dot_general(
                m[off:, :], m[off:off + 128, :], (((1,), (1,)), ((), ())),
                precision=HI, preferred_element_type=F32)


def chol_solve(g, p):
    return pl.pallas_call(
        chol_kernel,
        out_shape=jax.ShapeDtypeStruct((192, 512), F32),
        in_specs=[pl.BlockSpec(memory_space=pltpu.VMEM)] * 2,
        out_specs=pl.BlockSpec(memory_space=pltpu.VMEM),
        scratch_shapes=[pltpu.VMEM((704, 512), F32)],
        compiler_params=pltpu.CompilerParams(vmem_limit_bytes=32 * 2**20),
    )(g, p)


def on_device(activations, prev_basis):
    panel, gram = panel_and_gram(activations, prev_basis)
    return chol_solve(gram, panel)


def solution(mesh):
    in_specs = (P(None, ("dp", "seq"), None), P())
    out_specs = P("seq", None)
    return jax.shard_map(
        on_device, mesh=mesh, in_specs=in_specs, out_specs=out_specs, check_vma=False
    )
```

time: 379 us -> 106 us (0.28)
  the two profiles are of different devices: /device:TPU:6 before, /device:TPU:1 now
where the time goes in v2:
time: 106 us
  Pallas kernels  104 us (98%)
  local copies, waits for them, and re-layouts  2.21 us (2%)
    pallas_call x1, Pallas kernels, panel_and_gram(): pl.pallas_call(kernel, out_shape=(jax.ShapeDtypeStruct((NC, NX, 48, 256),...  77.2 us
    pallas_call x1, Pallas kernels, chol_solve(): pl.pallas_call(chol_kernel, out_shape=jax.ShapeDtypeStruct((192, 512), F3...  26.5 us
    unnamed x4, local copies, waits for them, and re-layouts  2.21 us

profile of v2, /device:TPU:1, one launch (start us, length us, event | category | flops | bytes accessed | tf_op | source)
XLA Modules:
  0.0 105.9 jit_solution(12598166880677023655)
XLA Ops:
  0.0 77.2 %shard_map.28 = (f32[2,4,48,256]{3,2,1,0:T(8,128)}, f32[2,4,8,8,512]{4,3,2,1,0:T(8,128)}) custom-call(bf16[4,64,6144]{2,1,0:T(8,128)(2,1)} %act.1, bf16[4,1536,512]{2,1,0:T(8,128)(2,1)} %basis.1), custom_call_target="tpu_custom_call" | custom-call | tf_op jit(solution)/shard_map/pallas_call | solution.py:245
  77.2 0.0 copy-start
  77.2 1.2 %copy-done = f32[2,4,8,8,512]{4,3,2,1,0:T(8,128)S(1)} copy-done((f32[2,4,8,8,512]{4,3,2,1,0:T(8,128)S(1)}, f32[2,4,8,8,512]{4,3,2,1,0:T(8,128)}, u32[]{:S(2)}) %copy-start) | copy-done | bytes 1048600
  78.5 0.0 copy-start.1
  78.5 1.0 copy-done.1
  79.5 26.5 %shard_map.29 = f32[192,512]{1,0:T(8,128)} custom-call(f32[2,4,8,8,512]{4,3,2,1,0:T(8,128)S(1)} %copy-done, f32[2,4,48,256]{3,2,1,0:T(8,128)S(1)} %copy-done.1), custom_call_target="tpu_custom_call" | custom-call | tf_op jit(solution)/shard_map/pallas_call | solution.py:332
Async XLA Ops:
  77.2 1.2 %copy-start = (f32[2,4,8,8,512]{4,3,2,1,0:T(8,128)S(1)}, f32[2,4,8,8,512]{4,3,2,1,0:T(8,128)}, u32[]{:S(2)}) copy-start(f32[2,4,8,8,512]{4,3,2,1,0:T(8,128)} %get-tuple-element.7.g_ref) | copy-start | bytes 3145732
  78.5 1.0 copy-start.1

commit v3 on v2

v3 whole, which is shorter than its diff:
```python
import math

import jax
import jax.numpy as jnp
from jax import lax
from jax.experimental import pallas as pl
from jax.experimental.pallas import tpu as pltpu
from jax.sharding import PartitionSpec as P

F32, BF16 = jnp.float32, jnp.bfloat16
NX, NC, NZ, NY, NB = 4, 2, 8, 4, 4
HI = lax.Precision.HIGHEST
STAGES = (("z", "y", "x"), ("y", "x", "z"), ("x", "z", "y"))
SIZE = {"x": NX, "y": NY, "z": NZ}


def splat_lane(v, k):
    return jnp.broadcast_to(v[:, k:k + 1], (8, 128))


def splat_row(v, k):
    return jnp.broadcast_to(v[k:k + 1, :], (8, 128))


def diag_inverse(a, between):
    n = len(a)
    sub = lax.broadcasted_iota(jnp.int32, (8, 128), 0)
    lane = lax.broadcasted_iota(jnp.int32, (8, 128), 1)
    out = []
    col = [splat_lane(a[0], j) for j in range(8)]
    for s in range(n):
        c0 = 8 * s
        r = a[s]
        ahead = s + 1 < n
        if ahead:
            ncol = [splat_lane(a[s + 1], c0 + j) for j in range(8)]
        inv_rows = jnp.zeros((8, 128), F32)
        factors = []
        for k in range(8):
            inv = 1.0 / splat_row(col[k], k)
            inv_rows = jnp.where(sub == k, inv, inv_rows)
            m = jnp.where(sub > k, col[k] * inv, 0.0)
            if ahead:
                factors.append(ncol[k] * inv)
            if k < 7:
                row = jnp.where(lane == c0 + k, 1.0, splat_row(r, k))
                r = jnp.where((lane == c0 + k) & (sub > k), 0.0, r) - m * row
                for j in range(k + 1, 8):
                    top = splat_row(col[j], k)
                    col[j] = col[j] - m * top
                    if ahead:
                        ncol[j] = ncol[j] - factors[k] * top
        rel = lane - c0 - sub
        rp = jnp.where(rel == 0, 1.0, jnp.where((rel > 0) & (lane < c0 + 8), 0.0, r))
        out.append(jnp.where(lane < c0 + 8, rp, 0.0) * jnp.sqrt(inv_rows))
        strip = (lane >= c0) & (lane < c0 + 8)
        if ahead:
            acc = jnp.where(strip, 0.0, a[s + 1])
            for k in range(8):
                acc = acc - factors[k] * splat_row(rp, k)
            a[s + 1] = acc
            col = [splat_lane(acc, c0 + 8 + j) for j in range(8)]
        if s + 2 < n:
            ut = (r * inv_rows).T
            for t in range(s + 2, n):
                mult = ut[8 * t:8 * t + 8, :]
                acc = jnp.where(strip, 0.0, a[t])
                for k in range(8):
                    acc = acc - splat_lane(mult, k) * splat_row(rp, k)
                a[t] = acc
        between(s)
    return out


class Copies:
    def __init__(self, send_sems, recv_sems):
        self.send_sems, self.recv_sems, self.count, self.made = send_sems, recv_sems, 0, []

    def send(self, src, dst, device):
        n = self.count
        self.count += 1
        copy = pltpu.make_async_remote_copy(
            src_ref=src, dst_ref=dst, send_sem=self.send_sems.at[n], recv_sem=self.recv_sems.at[n],
            device_id=device, device_id_type=pl.DeviceIdType.MESH,
        )
        copy.start()
        self.made.append(copy)
        return copy


def ring(copies, n, me, piece, half, to, up_s, up_r, dn_s, dn_r, up_h, dn_h, up_hr, dn_hr):
    steps = n // 2
    far = piece(lax.rem(me + steps, n))
    up_h[...] = far[:half].astype(BF16)
    dn_h[...] = far[half:].astype(BF16)
    up = copies.send(up_h, up_hr, to(lax.rem(me + 1, n)))
    dn = copies.send(dn_h, dn_hr, to(lax.rem(me + n - 1, n)))
    yield
    for i in range(1, steps):
        d = steps - i
        mine = piece(lax.rem(me + d, n))
        up.wait_recv()
        if i == 1:
            up_s[0, :half] = (mine[:half] + up_hr[...].astype(F32)).astype(BF16)
            up_s[0, half:] = mine[half:].astype(BF16)
        else:
            up_s[i - 1] = (mine + up_r[i - 2].astype(F32)).astype(BF16)
        up = copies.send(up_s.at[i - 1], up_r.at[i - 1], to(lax.rem(me + 1, n)))
        mine = piece(lax.rem(me + n - d, n))
        dn.wait_recv()
        if i == 1:
            dn_s[0, half:] = (mine[half:] + dn_hr[...].astype(F32)).astype(BF16)
            dn_s[0, :half] = mine[:half].astype(BF16)
        else:
            dn_s[i - 1] = (mine + dn_r[i - 2].astype(F32)).astype(BF16)
        dn = copies.send(dn_s.at[i - 1], dn_r.at[i - 1], to(lax.rem(me + n - 1, n)))
        yield
    up.wait_recv()
    dn.wait_recv()
    return piece(me) + up_r[steps - 2].astype(F32) + dn_r[steps - 2].astype(F32)


def direct(copies, n, me, piece, to, bufs, bufr):
    sent = []
    for d in range(1, n):
        bufs[d - 1] = piece(lax.rem(me + d, n)).astype(bufs.dtype)
        sent.append(copies.send(bufs.at[d - 1], bufr.at[d - 1], to(lax.rem(me + d, n))))
    yield
    total = piece(me)
    for d in range(1, n):
        sent[d - 1].wait_recv()
        total = total + bufr[d - 1].astype(F32)
    return total


def kernel(act, basis, out, *scratch):
    (a_v, b_v, proj, pan, p_v, g_v, gs, gr, up, rows_v, out_v, load_sems, send_sems, recv_sems, out_sems,
     *bufs) = scratch
    bufs = list(bufs)
    dp, seq = lax.axis_index("dp"), lax.axis_index("seq")
    x, c, z, y = dp // 2, lax.rem(dp, 2), seq // NY, lax.rem(seq, NY)
    zz = lax.rem(z, 2)
    me = {"x": x, "y": y, "z": z}

    def dev(x_=None, c_=None, z_=None, y_=None):
        x_, c_, z_, y_ = (x if x_ is None else x_, c if c_ is None else c_,
                          z if z_ is None else z_, y if y_ is None else y_)
        return (x_ * NC + c_, z_ * NY + y_)

    peers = [dev(c_=1 - c)]
    for d in range(1, NX):
        peers.append(dev(x_=lax.rem(x + d, NX)))
    for d in range(1, NY):
        peers += [dev(y_=lax.rem(y + d, NY)), dev(z_=z + 1 - 2 * zz, y_=lax.rem(y + d, NY))]
    for d in range(1, NZ):
        peers.append(dev(z_=lax.rem(z + d, NZ)))
    barrier = pltpu.get_barrier_semaphore()
    for peer in peers:
        pl.semaphore_signal(barrier, inc=1, device_id=peer, device_id_type=pl.DeviceIdType.MESH)

    order = [lax.rem(z // 2 + o, 4) for o in (2, 1, 3, 0)]
    own_loads, b_loads = [], []
    for i, j in enumerate(order):
        cols = pl.ds(pl.multiple_of(j * 1536, 1536), 1536)
        b_loads.append(pltpu.make_async_copy(
            basis.at[j, :, pl.ds(pl.multiple_of(c * 256, 256), 256)], b_v.at[i], load_sems.at[i]))
        own_loads.append(pltpu.make_async_copy(act.at[:, :, cols], a_v.at[i, 0], load_sems.at[4 + i]))
        own_loads[i].start()
        b_loads[i].start()

    pl.semaphore_wait(barrier, len(peers))

    copies = Copies(send_sems, recv_sems)
    exchanged = []
    for i, j in enumerate(order):
        cols = pl.ds(pl.multiple_of(j * 1536, 1536), 1536)
        exchanged.append(copies.send(act.at[:, :, cols], a_v.at[i, 1], dev(c_=1 - c)))

    def first(t, sub, pool):
        axis = STAGES[t][0]
        if t == 0:
            view, pos = pan.at[0, :, 2 * sub:2 * sub + 2], 0
        else:
            view, pos = pan.at[t, pl.ds(2 * order[sub], 2)], t

        def piece(dest):
            return view[(slice(None),) * pos + (dest,)]

        def to(dest):
            return dev(**{axis + "_": dest})

        total = yield from ring(copies, SIZE[axis], me[axis], piece, 1, to, *pool[:8])
        if t == 0:
            mid[0][2 * sub:2 * sub + 2] = total
        else:
            mid[t][pl.ds(2 * order[sub], 2)] = total

    def rest(t, pool):
        left = [a for a in ("z", "y", "x") if a != STAGES[t][0]]
        cur = mid[t]
        for stage in (1, 2):
            axis = STAGES[t][stage]
            pos = left.index(axis)
            left.pop(pos)

            def piece(dest, cur=cur, pos=pos):
                return cur[(slice(None),) * pos + (dest,)]

            def to(dest, axis=axis):
                return dev(**{axis + "_": dest})

            total = yield from direct(copies, SIZE[axis], me[axis], piece, to, pool[0], pool[1])
            if stage == 1:
                cur = pool[2]
                cur[...] = total
                pool = pool[3:]
            else:
                p_v[c, x, 16 * t:16 * t + 16, :] = total * (1.0 / 65536.0)

    mid = [bufs.pop(0) for _ in range(3)]
    rings = []
    for t in range(3):
        subs = []
        for sub in range(2 if t == 0 else 4):
            subs.append(first(t, sub, bufs[:8]))
            bufs = bufs[8:]
        rings.append(subs)
    rests = []
    for t in range(3):
        rests.append(rest(t, bufs[:5]))
        bufs = bufs[5:]

    def step(gen):
        try:
            next(gen)
            return True
        except StopIteration:
            return False

    def compute(i):
        j = order[i]
        b_loads[i].wait()
        own_loads[i].wait()
        proj[0:256, :] = jnp.dot(a_v[i, 0].reshape(256, 1536), b_v[i], preferred_element_type=F32).astype(BF16)
        exchanged[i].wait_recv()
        proj[256:512, :] = jnp.dot(a_v[i, 1].reshape(256, 1536), b_v[i], preferred_element_type=F32).astype(BF16)
        for k in range(4):
            lhs = a_v[i, :, :, :, 384 * k:384 * k + 384].reshape(512, 384)
            r = lax.dot_general(lhs, proj[...], (((0,), (0,)), ((), ())), preferred_element_type=F32)
            r = r.reshape(2, 4, 3, 16, 256)
            for t in range(3):
                pan[t, 2 * j + k // 2, 2 * (k % 2):2 * (k % 2) + 2] = r[:, :, t]

    compute(0)
    step(rings[0][0])
    step(rings[0][1])
    step(rings[1][0])
    step(rings[2][0])
    compute(1)
    step(rings[1][1])
    step(rings[2][1])
    compute(2)
    step(rings[1][2])
    step(rings[2][2])
    step(rings[0][0])
    step(rings[0][1])
    step(rings[1][0])
    step(rings[2][0])
    compute(3)
    step(rings[1][3])
    step(rings[2][3])
    step(rings[1][1])
    step(rings[2][1])
    step(rings[0][0])
    step(rings[0][1])
    step(rings[1][2])
    step(rings[2][2])
    step(rings[1][0])
    step(rings[2][0])
    step(rings[0][0])
    step(rings[0][1])
    step(rings[1][3])
    step(rings[2][3])
    for sub in range(1, 4):
        step(rings[1][sub])
        step(rings[2][sub])
    step(rests[2])
    step(rests[1])
    step(rings[0][0])
    step(rings[0][1])
    step(rests[0])

    step(rests[1])
    step(rests[0])
    step(rests[2])
    step(rests[0])
    step(rests[1])
    step(rests[2])

    sent = []
    for d in range(1, NX):
        sent.append(copies.send(p_v.at[c, x], p_v.at[c, x], dev(x_=lax.rem(x + d, NX))))
    swap = copies.send(p_v.at[c, x], p_v.at[c, x], dev(c_=1 - c))
    passed = [swap]
    for d in range(1, NX):
        sent[d - 1].wait_recv()
        other = lax.rem(x + NX - d, NX)
        passed.append(copies.send(p_v.at[c, other], p_v.at[c, other], dev(c_=1 - c)))
    for copy in passed:
        copy.wait_recv()

    for h in range(2):
        rows_v[:, 256 * h:256 * h + 256] = p_v[h].reshape(192, 256)
    for b in range(NB):
        lo = 128 * b
        gs[b, :, :, :, lo:] = lax.dot_general(
            rows_v[:, lo:lo + 128], rows_v[:, lo:], (((0,), (0,)), ((), ())), precision=HI,
            preferred_element_type=F32).reshape(8, 2, 8, 512 - lo)
    q_me = c * NX + x
    p_me = zz * NY + y
    parts = (pl.ds(0, 1), pl.ds(1, NB - 1))

    def peer(d):
        q = lax.rem(p_me + d, 8)
        return q, dev(z_=z - zz + q // NY, y_=lax.rem(q, NY))

    def cols(p):
        return pl.ds(pl.multiple_of(lax.rem(p, NB) * 128, 128), 128)

    reduced = [[], []]
    for h, part in enumerate(parts):
        for d in range(1, 8):
            p, to = peer(d)
            reduced[h].append(copies.send(
                gs.at[part, q_me, p // NB, :, cols(p)], gr.at[d - 1, part], to))
    spread = [[], []]
    for h, part in enumerate(parts):
        total = gs[part, q_me, p_me // NB, :, cols(p_me)]
        for d in range(1, 8):
            reduced[h][d - 1].wait_recv()
            total = total + gr[d - 1, part]
        g_v[part, c, x, p_me] = total
        for d in range(1, 8):
            mine = g_v.at[part, c, x, p_me]
            spread[h].append(copies.send(mine, mine, peer(d)[1]))
    across = [[], []]
    for h, part in enumerate(parts):
        for copy in spread[h]:
            copy.wait_recv()
        for d in range(1, NX):
            mine = g_v.at[part, c, x]
            across[h].append(copies.send(mine, mine, dev(x_=lax.rem(x + d, NX))))
    swapped = [None, None]

    def swap_cores(h):
        for copy in across[h]:
            copy.wait_recv()
        mine = g_v.at[parts[h], c]
        swapped[h] = copies.send(mine, mine, dev(c_=1 - c))

    def arrive(h):
        swapped[h].wait_recv()
        for b in range(1) if h == 0 else range(1, NB):
            for q in range(8):
                for rt in range(2):
                    for ct in range(b, NB):
                        up[b, 16 * q + 8 * rt:16 * q + 8 * rt + 8, 128 * ct:128 * ct + 128] = (
                            g_v[b, q // NX, q % NX, NB * rt + ct])

    swap_cores(0)
    arrive(0)
    written = []
    for b in range(NB):
        lo, hi = 128 * b, 128 * b + 128

        def between(strip):
            if b == 0 and strip == 7:
                swap_cores(1)

        inv = jnp.concatenate(
            diag_inverse([up[b, 8 * i:8 * i + 8, lo:hi] for i in range(16)], between), axis=0)
        if b == 0:
            arrive(1)
        if b < NB - 1:
            u = jnp.dot(inv, up[b, :, hi:], precision=HI, preferred_element_type=F32)
            for e in range(b + 1, NB):
                off = 128 * (e - b - 1)
                up[e, :, 128 * e:] -= lax.dot_general(
                    u[:, off:off + 128], u[:, off:], (((0,), (0,)), ((), ())), precision=HI,
                    preferred_element_type=F32)
        solved = lax.dot_general(rows_v[:, lo:hi], inv, (((1,), (1,)), ((), ())), precision=HI,
                                 preferred_element_type=F32)
        out_v[:, lo:hi] = solved * math.sqrt(1536.0)
        written.append(pltpu.make_async_copy(out_v.at[:, lo:hi], out.at[:, lo:hi], out_sems.at[b]))
        written[b].start()
        if b < NB - 1:
            rows_v[:, hi:] -= jnp.dot(solved, u, precision=HI, preferred_element_type=F32)
    for copy in copies.made:
        copy.wait_send()
    for copy in written:
        copy.wait()


def refreshed(act, basis):
    tile = (16, 256)
    mids, firsts, rests = [], [], []
    for t, axes in enumerate(STAGES):
        left = [a for a in ("z", "y", "x") if a != axes[0]]
        mids.append(pltpu.VMEM(tuple(SIZE[a] for a in left) + tile, F32))
        steps = SIZE[axes[0]] // 2
        full = (2, 4) + tile
        for _ in range(2 if t == 0 else 4):
            firsts += [pltpu.VMEM((steps - 1,) + full, BF16)] * 4 + [pltpu.VMEM((1,) + full[1:], BF16)] * 4
        left.remove(axes[1])
        shape = (SIZE[left[0]],) + tile
        rests += [pltpu.VMEM((SIZE[axes[1]] - 1,) + shape, BF16)] * 2 + [pltpu.VMEM(shape, F32)]
        rests += [pltpu.VMEM((SIZE[axes[2]] - 1,) + tile, F32)] * 2
    bufs = mids + firsts + rests
    return pl.pallas_call(
        kernel,
        out_shape=jax.ShapeDtypeStruct((192, 512), F32),
        in_specs=[pl.BlockSpec(memory_space=pl.ANY)] * 2,
        out_specs=pl.BlockSpec(memory_space=pl.ANY),
        scratch_shapes=[
            pltpu.VMEM((4, 2, 4, 64, 1536), BF16),
            pltpu.VMEM((4, 1536, 256), BF16),
            pltpu.VMEM((512, 256), BF16),
            pltpu.VMEM((3, NZ, NY, NX, 16, 256), F32),
            pltpu.VMEM((NC, NX, 48, 256), F32),
            pltpu.VMEM((NB, NC, NX, 8, 8, 128), F32),
            pltpu.VMEM((NB, 8, 2, 8, 512), F32),
            pltpu.VMEM((7, NB, 8, 128), F32),
            pltpu.VMEM((NB, 128, 512), F32),
            pltpu.VMEM((192, 512), F32),
            pltpu.VMEM((192, 512), F32),
            pltpu.SemaphoreType.DMA((8,)),
            pltpu.SemaphoreType.DMA((128,)),
            pltpu.SemaphoreType.DMA((128,)),
            pltpu.SemaphoreType.DMA((4,)),
        ] + bufs,
        compiler_params=pltpu.CompilerParams(
            collective_id=1, has_side_effects=True, vmem_limit_bytes=56 * 2**20),
    )(act, basis)


def on_device(activations, prev_basis):
    return refreshed(activations, prev_basis)


def solution(mesh):
    in_specs = (P(None, ("dp", "seq"), None), P())
    out_specs = P("seq", None)
    return jax.shard_map(
        on_device, mesh=mesh, in_specs=in_specs, out_specs=out_specs, check_vma=False
    )
```

time: 106 us -> 88.4 us (0.83)
  Pallas kernels: 104 us -> 86.5 us
    pallas_call x2 -> x1, Pallas kernels: 104 us -> 86.5 us  [refreshed(): pl.pallas_call(kernel, out_shape=jax.ShapeDtypeStruct((192, 512), F32), i...]
    unnamed x4 -> x1, local copies, waits for them, and re-layouts: 2.21 us -> 1.77 us
where the time goes in v3:
time: 88.4 us; the launch traced here: 88.3 us
  Pallas kernels  86.5 us (98%)
  local copies, waits for them, and re-layouts  1.77 us (2%)
    pallas_call x1, Pallas kernels, refreshed(): pl.pallas_call(kernel, out_shape=jax.ShapeDtypeStruct((192, 512), F32), i...  86.5 us

profile of v3, /device:TPU:1, one launch (start us, length us, event | category | flops | bytes accessed | tf_op | source)
XLA Modules:
  0.0 88.3 jit_solution(12839735834990985350)
XLA Ops:
  0.0 86.5 %shard_map.28 = f32[192,512]{1,0:T(8,128)} custom-call(bf16[4,64,6144]{2,1,0:T(8,128)(2,1)} %act.1, bf16[4,1536,512]{2,1,0:T(8,128)(2,1)} %basis.1), custom_call_target="tpu_custom_call" | custom-call | tf_op jit(solution)/shard_map/pallas_call | solution.py:419
  86.5 1.8 %copy.4 = f32[192,512]{1,0:T(8,128)} copy(f32[192,512]{1,0:T(8,128)} %shard_map.28) | data formatting | bytes 786432

commit v4 on v3

--- a/solution.py
+++ b/solution.py
@@ -1,3 +1,4 @@
+import functools
 import math
 
 import jax
@@ -10,7 +11,7 @@
 F32, BF16 = jnp.float32, jnp.bfloat16
 NX, NC, NZ, NY, NB = 4, 2, 8, 4, 4
 HI = lax.Precision.HIGHEST
-STAGES = (("z", "y", "x"), ("y", "x", "z"), ("x", "z", "y"))
+STAGES = (("z", "y", "x"), ("y", "x", "z"), ("x", "y", "z"))
 SIZE = {"x": NX, "y": NY, "z": NZ}
 
 
@@ -20,6 +21,13 @@
 
 def splat_row(v, k):
     return jnp.broadcast_to(v[k:k + 1, :], (8, 128))
+
+
+def three_terms(v):
+    high = v.astype(BF16).astype(F32)
+    left = v - high
+    middle = left.astype(BF16).astype(F32)
+    return high, middle, left - middle
 
 
 def diag_inverse(a, between):
@@ -61,13 +69,13 @@
             a[s + 1] = acc
             col = [splat_lane(acc, c0 + 8 + j) for j in range(8)]
         if s + 2 < n:
-            ut = (r * inv_rows).T
+            uh, um, ul = three_terms(r * inv_rows)
+            rh, rm, rl = three_terms(rp)
+            left = jnp.concatenate([uh, uh, um, uh, ul, um], axis=0).astype(BF16)
+            right = jnp.concatenate([rh, rm, rh, rl, rh, rm], axis=0).astype(BF16)
+            update = lax.dot_general(left, right, (((0,), (0,)), ((), ())), preferred_element_type=F32)
             for t in range(s + 2, n):
-                mult = ut[8 * t:8 * t + 8, :]
-                acc = jnp.where(strip, 0.0, a[t])
-                for k in range(8):
-                    acc = acc - splat_lane(mult, k) * splat_row(rp, k)
-                a[t] = acc
+                a[t] = jnp.where(strip, 0.0, a[t]) - update[8 * t:8 * t + 8, :]
         between(s)
     return out
 
@@ -289,13 +297,12 @@
     step(rings[0][0])
     step(rings[0][1])
     step(rests[0])
-
     step(rests[1])
-    step(rests[0])
     step(rests[2])
     step(rests[0])
     step(rests[1])
     step(rests[2])
+    step(rests[0])
 
     sent = []
     for d in range(1, NX):
@@ -311,11 +318,12 @@
 
     for h in range(2):
         rows_v[:, 256 * h:256 * h + 256] = p_v[h].reshape(192, 256)
-    for b in range(NB):
+    def gram(b):
         lo = 128 * b
         gs[b, :, :, :, lo:] = lax.dot_general(
             rows_v[:, lo:lo + 128], rows_v[:, lo:], (((0,), (0,)), ((), ())), precision=HI,
             preferred_element_type=F32).reshape(8, 2, 8, 512 - lo)
+
     q_me = c * NX + x
     p_me = zz * NY + y
     parts = (pl.ds(0, 1), pl.ds(1, NB - 1))
@@ -329,6 +337,8 @@
 
     reduced = [[], []]
     for h, part in enumerate(parts):
+        for b in range(1) if h == 0 else range(1, NB):
+            gram(b)
         for d in range(1, 8):
             p, to = peer(d)
             reduced[h].append(copies.send(
@@ -339,48 +349,61 @@
         for d in range(1, 8):
             reduced[h][d - 1].wait_recv()
             total = total + gr[d - 1, part]
-        g_v[part, c, x, p_me] = total
+        g_v[part, c, x, p_me // NB, lax.rem(p_me, NB)] = total
         for d in range(1, 8):
-            mine = g_v.at[part, c, x, p_me]
+            mine = g_v.at[part, c, x, p_me // NB, lax.rem(p_me, NB)]
             spread[h].append(copies.send(mine, mine, peer(d)[1]))
-    across = [[], []]
-    for h, part in enumerate(parts):
-        for copy in spread[h]:
+    diagonal, across, swapped = [], [[] for _ in range(NB)], []
+
+    def spread_x(b):
+        for d in range(1, NX):
+            mine = g_v.at[b, c, x, :, max(b, 1):]
+            across[b].append(copies.send(mine, mine, dev(x_=lax.rem(x + d, NX))))
+
+    for copy in spread[0]:
+        copy.wait_recv()
+    for d in range(1, 8):
+        mine = g_v.at[0, c, x, :, 0]
+        diagonal.append(copies.send(
+            mine, mine, dev(x_=lax.rem(x + d // 2, NX), c_=c if d % 2 == 0 else 1 - c)))
+    spread_x(0)
+    for copy in spread[1]:
+        copy.wait_recv()
+    for b in range(1, NB):
+        spread_x(b)
+
+    def swap_cores(b):
+        for copy in across[b]:
             copy.wait_recv()
-        for d in range(1, NX):
-            mine = g_v.at[part, c, x]
-            across[h].append(copies.send(mine, mine, dev(x_=lax.rem(x + d, NX))))
-    swapped = [None, None]
-
-    def swap_cores(h):
-        for copy in across[h]:
-            copy.wait_recv()
-        mine = g_v.at[parts[h], c]
-        swapped[h] = copies.send(mine, mine, dev(c_=1 - c))
-
-    def arrive(h):
-        swapped[h].wait_recv()
-        for b in range(1) if h == 0 else range(1, NB):
-            for q in range(8):
-                for rt in range(2):
-                    for ct in range(b, NB):
-                        up[b, 16 * q + 8 * rt:16 * q + 8 * rt + 8, 128 * ct:128 * ct + 128] = (
-                            g_v[b, q // NX, q % NX, NB * rt + ct])
-
-    swap_cores(0)
-    arrive(0)
-    written = []
+        mine = g_v.at[b, c, :, :, max(b, 1):]
+        swapped.append(copies.send(mine, mine, dev(c_=1 - c)))
+
+    def take(b, first, last):
+        for q in range(8):
+            for rt in range(2):
+                for ct in range(first, last):
+                    up[b, 16 * q + 8 * rt:16 * q + 8 * rt + 8, 128 * ct:128 * ct + 128] = (
+                        g_v[b, q // NX, q % NX, rt, ct])
+
+    def arrive(b):
+        swapped[b].wait_recv()
+        take(b, max(b, 1), NB)
+
+    for copy in diagonal:
+        copy.wait_recv()
+    take(0, 0, 1)
     for b in range(NB):
         lo, hi = 128 * b, 128 * b + 128
 
         def between(strip):
-            if b == 0 and strip == 7:
-                swap_cores(1)
+            if b == 0 and strip in (3, 5, 8, 9):
+                swap_cores((3, 5, 8, 9).index(strip))
 
         inv = jnp.concatenate(
             diag_inverse([up[b, 8 * i:8 * i + 8, lo:hi] for i in range(16)], between), axis=0)
         if b == 0:
-            arrive(1)
+            for e in range(NB):
+                arrive(e)
         if b < NB - 1:
             u = jnp.dot(inv, up[b, :, hi:], precision=HI, preferred_element_type=F32)
             for e in range(b + 1, NB):
@@ -391,14 +414,13 @@
         solved = lax.dot_general(rows_v[:, lo:hi], inv, (((1,), (1,)), ((), ())), precision=HI,
                                  preferred_element_type=F32)
         out_v[:, lo:hi] = solved * math.sqrt(1536.0)
-        written.append(pltpu.make_async_copy(out_v.at[:, lo:hi], out.at[:, lo:hi], out_sems.at[b]))
-        written[b].start()
         if b < NB - 1:
             rows_v[:, hi:] -= jnp.dot(solved, u, precision=HI, preferred_element_type=F32)
+    written = pltpu.make_async_copy(out_v, out, out_sems.at[0])
+    written.start()
     for copy in copies.made:
         copy.wait_send()
-    for copy in written:
-        copy.wait()
+    written.wait()
 
 
 def refreshed(act, basis):
@@ -427,16 +449,16 @@
             pltpu.VMEM((512, 256), BF16),
             pltpu.VMEM((3, NZ, NY, NX, 16, 256), F32),
             pltpu.VMEM((NC, NX, 48, 256), F32),
-            pltpu.VMEM((NB, NC, NX, 8, 8, 128), F32),
+            pltpu.VMEM((NB, NC, NX, 2, NB, 8, 128), F32),
             pltpu.VMEM((NB, 8, 2, 8, 512), F32),
             pltpu.VMEM((7, NB, 8, 128), F32),
             pltpu.VMEM((NB, 128, 512), F32),
             pltpu.VMEM((192, 512), F32),
             pltpu.VMEM((192, 512), F32),
             pltpu.SemaphoreType.DMA((8,)),
-            pltpu.SemaphoreType.DMA((128,)),
-            pltpu.SemaphoreType.DMA((128,)),
-            pltpu.SemaphoreType.DMA((4,)),
+            pltpu.SemaphoreType.DMA((192,)),
+            pltpu.SemaphoreType.DMA((192,)),
+            pltpu.SemaphoreType.DMA((1,)),
         ] + bufs,
         compiler_params=pltpu.CompilerParams(
             collective_id=1, has_side_effects=True, vmem_limit_bytes=56 * 2**20),

time: 88.4 us -> 85.4 us (0.966)
  Pallas kernels: 86.5 us -> 83.5 us
    pallas_call x1, Pallas kernels: 86.5 us -> 83.5 us  [refreshed(): pl.pallas_call(kernel, out_shape=jax.ShapeDtypeStruct((192, 512), F32), i...]
where the time goes in v4:
time: 85.4 us; the launch traced here: 85.3 us
  Pallas kernels  83.5 us (98%)
  local copies, waits for them, and re-layouts  1.77 us (2%)
    pallas_call x1, Pallas kernels, refreshed(): pl.pallas_call(kernel, out_shape=jax.ShapeDtypeStruct((192, 512), F32), i...  83.5 us
    unnamed x1, local copies, waits for them, and re-layouts  1.77 us

profile of v4, /device:TPU:1, one launch (start us, length us, event | category | flops | bytes accessed | tf_op | source)
XLA Modules:
  0.0 85.3 jit_solution(634827819448437449)
XLA Ops:
  0.0 83.5 %shard_map.28 = f32[192,512]{1,0:T(8,128)} custom-call(bf16[4,64,6144]{2,1,0:T(8,128)(2,1)} %act.1, bf16[4,1536,512]{2,1,0:T(8,128)(2,1)} %basis.1), custom_call_target="tpu_custom_call" | custom-call | tf_op jit(solution)/shard_map/pallas_call | solution.py:441
  83.5 1.8 %copy.4 = f32[192,512]{1,0:T(8,128)} copy(f32[192,512]{1,0:T(8,128)} %shard_map.28) | data formatting | bytes 786432

commit v5 on v4

--- a/solution.py
+++ b/solution.py
@@ -84,13 +84,18 @@
     def __init__(self, send_sems, recv_sems):
         self.send_sems, self.recv_sems, self.count, self.made = send_sems, recv_sems, 0, []
 
-    def send(self, src, dst, device):
-        n = self.count
-        self.count += 1
-        copy = pltpu.make_async_remote_copy(
+    def take(self, number):
+        self.count += number
+        return self.count - number
+
+    def make(self, src, dst, device, n):
+        return pltpu.make_async_remote_copy(
             src_ref=src, dst_ref=dst, send_sem=self.send_sems.at[n], recv_sem=self.recv_sems.at[n],
             device_id=device, device_id_type=pl.DeviceIdType.MESH,
         )
+
+    def send(self, src, dst, device):
+        copy = self.make(src, dst, device, self.take(1))
         copy.start()
         self.made.append(copy)
         return copy
@@ -200,50 +205,50 @@
         total = yield from ring(copies, SIZE[axis], me[axis], piece, 1, to, *pool[:8])
         if t == 0:
             mid[0][2 * sub:2 * sub + 2] = total
+            return
+        j = order[sub]
+        mid[t][pl.ds(2 * j, 2)] = total
+        second = STAGES[t][1]
+        ready[t][pl.ds(2 * j, 2)] = yield from direct(
+            copies, SIZE[second], me[second], lambda dest: mid[t][pl.ds(2 * j, 2), dest],
+            lambda dest: dev(**{second + "_": dest}), *pool[8:])
+        for dest in (2 * j, 2 * j + 1) if sub < 3 else (2 * j + 1 - zz,):
+            d = lax.rem(dest - z + NZ, NZ)
+            copies.make(ready[t].at[dest], got[t].at[d - 1], dev(z_=dest), base[t] + d - 1).start()
+
+    def rest(t, pool):
+        if t == 0:
+            total = yield from direct(copies, NY, y, lambda d: mid[0][d], lambda d: dev(y_=d), *pool[0:2])
+            pool[2][...] = total
+            total = yield from direct(copies, NX, x, lambda d: pool[2][d], lambda d: dev(x_=d), *pool[3:5])
         else:
-            mid[t][pl.ds(2 * order[sub], 2)] = total
-
-    def rest(t, pool):
-        left = [a for a in ("z", "y", "x") if a != STAGES[t][0]]
-        cur = mid[t]
-        for stage in (1, 2):
-            axis = STAGES[t][stage]
-            pos = left.index(axis)
-            left.pop(pos)
-
-            def piece(dest, cur=cur, pos=pos):
-                return cur[(slice(None),) * pos + (dest,)]
-
-            def to(dest, axis=axis):
-                return dev(**{axis + "_": dest})
-
-            total = yield from direct(copies, SIZE[axis], me[axis], piece, to, pool[0], pool[1])
-            if stage == 1:
-                cur = pool[2]
-                cur[...] = total
-                pool = pool[3:]
-            else:
-                p_v[c, x, 16 * t:16 * t + 16, :] = total * (1.0 / 65536.0)
+            total = ready[t][z]
+            for d in range(1, NZ):
+                to = lax.rem(z + d, NZ)
+                copy = copies.make(ready[t].at[to], got[t].at[d - 1], dev(z_=to), base[t] + d - 1)
+                copy.wait_recv()
+                copies.made.append(copy)
+                total = total + got[t][d - 1]
+        p_v[c, x, 16 * t:16 * t + 16, :] = total * (1.0 / 65536.0)
 
     mid = [bufs.pop(0) for _ in range(3)]
+    ready = [None] + [bufs.pop(0) for _ in range(2)]
+    got = [None] + [bufs.pop(0) for _ in range(2)]
+    base = [None] + [copies.take(NZ - 1) for _ in range(2)]
     rings = []
     for t in range(3):
         subs = []
         for sub in range(2 if t == 0 else 4):
-            subs.append(first(t, sub, bufs[:8]))
-            bufs = bufs[8:]
+            size = 8 if t == 0 else 10
+            subs.append(first(t, sub, bufs[:size]))
+            bufs = bufs[size:]
         rings.append(subs)
-    rests = []
-    for t in range(3):
-        rests.append(rest(t, bufs[:5]))
-        bufs = bufs[5:]
-
-    def step(gen):
-        try:
-            next(gen)
-            return True
-        except StopIteration:
-            return False
+    rests = [rest(0, bufs), rest(1, ()), rest(2, ())]
+
+    def run(*names):
+        for name in names:
+            t, sub = name // 10, name % 10
+            next(rests[t] if sub == 9 else rings[t][sub], None)
 
     def compute(i):
         j = order[i]
@@ -260,49 +265,14 @@
                 pan[t, 2 * j + k // 2, 2 * (k % 2):2 * (k % 2) + 2] = r[:, :, t]
 
     compute(0)
-    step(rings[0][0])
-    step(rings[0][1])
-    step(rings[1][0])
-    step(rings[2][0])
+    run(0, 1, 10, 20)
     compute(1)
-    step(rings[1][1])
-    step(rings[2][1])
+    run(11, 21)
     compute(2)
-    step(rings[1][2])
-    step(rings[2][2])
-    step(rings[0][0])
-    step(rings[0][1])
-    step(rings[1][0])
-    step(rings[2][0])
+    run(12, 22, 0, 1, 10, 20)
     compute(3)
-    step(rings[1][3])
-    step(rings[2][3])
-    step(rings[1][1])
-    step(rings[2][1])
-    step(rings[0][0])
-    step(rings[0][1])
-    step(rings[1][2])
-    step(rings[2][2])
-    step(rings[1][0])
-    step(rings[2][0])
-    step(rings[0][0])
-    step(rings[0][1])
-    step(rings[1][3])
-    step(rings[2][3])
-    for sub in range(1, 4):
-        step(rings[1][sub])
-        step(rings[2][sub])
-    step(rests[2])
-    step(rests[1])
-    step(rings[0][0])
-    step(rings[0][1])
-    step(rests[0])
-    step(rests[1])
-    step(rests[2])
-    step(rests[0])
-    step(rests[1])
-    step(rests[2])
-    step(rests[0])
+    run(13, 23, 11, 21, 0, 1, 12, 22, 10, 20, 13, 23, 11, 21, 0, 1, 12, 22)
+    run(10, 20, 13, 23, 11, 21, 0, 1, 9, 12, 22, 13, 23, 9, 19, 29, 9)
 
     sent = []
     for d in range(1, NX):
@@ -425,19 +395,17 @@
 
 def refreshed(act, basis):
     tile = (16, 256)
-    mids, firsts, rests = [], [], []
+    bufs = [pltpu.VMEM((NY, NX) + tile, F32), pltpu.VMEM((NZ, NX) + tile, F32), pltpu.VMEM((NZ, NY) + tile, F32)]
+    bufs += [pltpu.VMEM((NZ,) + tile, F32)] * 2 + [pltpu.VMEM((NZ - 1,) + tile, F32)] * 2
     for t, axes in enumerate(STAGES):
-        left = [a for a in ("z", "y", "x") if a != axes[0]]
-        mids.append(pltpu.VMEM(tuple(SIZE[a] for a in left) + tile, F32))
         steps = SIZE[axes[0]] // 2
         full = (2, 4) + tile
         for _ in range(2 if t == 0 else 4):
-            firsts += [pltpu.VMEM((steps - 1,) + full, BF16)] * 4 + [pltpu.VMEM((1,) + full[1:], BF16)] * 4
-        left.remove(axes[1])
-        shape = (SIZE[left[0]],) + tile
-        rests += [pltpu.VMEM((SIZE[axes[1]] - 1,) + shape, BF16)] * 2 + [pltpu.VMEM(shape, F32)]
-        rests += [pltpu.VMEM((SIZE[axes[2]] - 1,) + tile, F32)] * 2
-    bufs = mids + firsts + rests
+            bufs += [pltpu.VMEM((steps - 1,) + full, BF16)] * 4 + [pltpu.VMEM((1,) + full[1:], BF16)] * 4
+            if t:
+                bufs += [pltpu.VMEM((3, 2) + tile, BF16)] * 2
+    bufs += [pltpu.VMEM((NY - 1, NX) + tile, BF16)] * 2 + [pltpu.VMEM((NX,) + tile, F32)]
+    bufs += [pltpu.VMEM((NX - 1,) + tile, F32)] * 2
     return pl.pallas_call(
         kernel,
         out_shape=jax.ShapeDtypeStruct((192, 512), F32),

time: 85.4 us -> 80.2 us (0.939)
  Pallas kernels: 83.5 us -> 78.3 us
    pallas_call x1, Pallas kernels: 83.5 us -> 78.3 us  [refreshed(): pl.pallas_call(kernel, out_shape=jax.ShapeDtypeStruct((192, 512), F32), i...]
where the time goes in v5:
time: 80.2 us; the launch traced here: 80.1 us
  Pallas kernels  78.3 us (98%)
  local copies, waits for them, and re-layouts  1.77 us (2%)
    pallas_call x1, Pallas kernels, refreshed(): pl.pallas_call(kernel, out_shape=jax.ShapeDtypeStruct((192, 512), F32), i...  78.3 us
    unnamed x1, local copies, waits for them, and re-layouts  1.77 us

profile of v5, /device:TPU:1, one launch (start us, length us, event | category | flops | bytes accessed | tf_op | source)
XLA Modules:
  0.0 80.1 jit_solution(484920108671888532)
XLA Ops:
  0.0 78.3 %shard_map.28 = f32[192,512]{1,0:T(8,128)} custom-call(bf16[4,64,6144]{2,1,0:T(8,128)(2,1)} %act.1, bf16[4,1536,512]{2,1,0:T(8,128)(2,1)} %basis.1), custom_call_target="tpu_custom_call" | custom-call | tf_op jit(solution)/shard_map/pallas_call | solution.py:409
  78.4 1.8 %copy.4 = f32[192,512]{1,0:T(8,128)} copy(f32[192,512]{1,0:T(8,128)} %shard_map.28) | data formatting | bytes 786432

commit v6 on v5

--- a/solution.py
+++ b/solution.py
@@ -366,8 +366,8 @@
         lo, hi = 128 * b, 128 * b + 128
 
         def between(strip):
-            if b == 0 and strip in (3, 5, 8, 9):
-                swap_cores((3, 5, 8, 9).index(strip))
+            if b == 0 and strip in (1, 2, 3, 4):
+                swap_cores((1, 2, 3, 4).index(strip))
 
         inv = jnp.concatenate(
             diag_inverse([up[b, 8 * i:8 * i + 8, lo:hi] for i in range(16)], between), axis=0)

time: 80.2 us -> 81 us (level)
  no operation moved by 1% of the time
where the time goes in v6:
time: 81 us; the launch traced here: 80.9 us
  Pallas kernels  79.1 us (98%)
  local copies, waits for them, and re-layouts  1.77 us (2%)
    pallas_call x1, Pallas kernels, refreshed(): pl.pallas_call(kernel, out_shape=jax.ShapeDtypeStruct((192, 512), F32), i...  79.1 us
    unnamed x1, local copies, waits for them, and re-layouts  1.77 us

profile of v6, /device:TPU:1, one launch (start us, length us, event | category | flops | bytes accessed | tf_op | source)
XLA Modules:
  0.0 80.9 jit_solution(17086215359197837797)
XLA Ops:
  0.0 79.1 %shard_map.28 = f32[192,512]{1,0:T(8,128)} custom-call(bf16[4,64,6144]{2,1,0:T(8,128)(2,1)} %act.1, bf16[4,1536,512]{2,1,0:T(8,128)(2,1)} %basis.1), custom_call_target="tpu_custom_call" | custom-call | tf_op jit(solution)/shard_map/pallas_call | solution.py:409
  79.1 1.8 %copy.4 = f32[192,512]{1,0:T(8,128)} copy(f32[192,512]{1,0:T(8,128)} %shard_map.28) | data formatting | bytes 786432
